TPU v7x, 32 devices: a whole 2x2x4 slice. The times are simulated.
32 devices in a mesh: col: 8 (over y, x, core), sec: 4 (over z).
Axes of the slice: x: 2, y: 2, z: 4, core: 2. Of those that a mesh axis runs over, the one named last changes fastest.
Arguments:
- couplings: float32 [2, 8, 3, 64, 512], P(None, 'col', None, None, 'sec'), may hold values from -0.625 to 0.625
- lower_sites: float32 [2, 8, 128, 128], P(None, 'col'), may hold values from -1.5 to 1.5
- left_edge: float32 [2, 8, 64, 128], P(None, 'sec'), may hold values from -6 to 6
- right_edge: float32 [2, 8, 64, 128], P(None, 'sec'), may hold values from -6 to 6
- bond_sizes: int32 [8, 8], P('col', 'sec'), may hold values from 1 to 64, as said below
Outputs:
- coupling_grad: float32 [2, 8, 3, 64, 512], P(None, 'col', None, None, 'sec')
Inputs may be any that keep to these rules, and one draw needn't show every extreme that they name: bond_sizes[c, q] is the number of live rows of sector q of the bond right of column c; some entry equals 64.
All inputs are finite; a program needn't handle non-finite values.
Results may differ from a plain program's by a relative error of at most 0.0003.
Values sent between devices are 32-bit elements; how exact they have to be, the bound alone decides.
A program may use at most 64 MiB of HBM per device.

v0:
```python
import math

import jax
import jax.numpy as jnp
from jax import lax
from jax.sharding import PartitionSpec as P

HIGHEST = lax.Precision.HIGHEST


def padded_2(block, sides, width):
    for axis, dim in sides:
        count = lax.axis_size(axis)
        forward = [(i, i + 1) for i in range(count - 1)]
        backward = [(target, source) for source, target in forward]
        low = lax.ppermute(
            lax.slice_in_dim(block, block.shape[dim] - width, None, axis=dim), axis, forward
        )
        high = lax.ppermute(lax.slice_in_dim(block, 0, width, axis=dim), axis, backward)
        block = jnp.concatenate([low, block, high], axis=dim)
    return block


def from_behind(array, axis, by):
    count = lax.axis_size(axis)
    pairs = [(i, i + by) for i in range(count) if 0 <= i + by < count]
    return lax.ppermute(array, axis, pairs)


def body(couplings, lower_sites, left_edge, right_edge, bond_sizes):
    row_count = couplings.shape[0]
    block_len = couplings.shape[3]
    sec_local = couplings.shape[4] // block_len
    bond_width = lower_sites.shape[3]
    col_count = lax.axis_size("col")
    column_index = lax.axis_index("col")
    turn_count = row_count + col_count - 1
    blocks_here = couplings[:, 0].reshape(row_count, 3, block_len, sec_local, block_len)
    lower_here = lower_sites[:, 0]
    positions = lax.broadcasted_iota(jnp.int32, (sec_local, block_len), 1)
    live_rows = (positions < bond_sizes[0][:, None]).astype(jnp.float32)[:, :, None]
    scale_factor = 1.0 / math.sqrt(bond_width)
    empty_env = jnp.zeros((sec_local, block_len, bond_width), jnp.float32)

    def advance(travel_env, blocks, lower):
        products = jnp.einsum("pikj,kjw->pkiw", blocks, travel_env, precision=HIGHEST)
        sideways = jnp.stack([products[2], products[0]], axis=1)
        padded = padded_2(sideways, (("sec", 0),), 1)
        summed = products[1] + padded[:sec_local, 0] + padded[2:, 1]
        return jnp.einsum("kiw,wv->kiv", summed, lower, precision=HIGHEST) * live_rows

    def retreat(padded, blocks):
        shifted = jnp.stack(
            [padded[0:sec_local], padded[1 : sec_local + 1], padded[2 : sec_local + 2]], axis=0
        )
        return jnp.einsum("pikj,pkiw->kjw", blocks, shifted, precision=HIGHEST)

    def left_turn(turn, state):
        travel_env, lefts = state
        row = turn - column_index
        active = (row >= 0) & (row < row_count)
        row_safe = jnp.clip(row, 0, row_count - 1)
        arriving = from_behind(travel_env, "col", 1)
        arriving = jnp.where(column_index == 0, left_edge[row_safe], arriving)
        record = jnp.where(active, arriving, lefts[row_safe])
        lefts = lax.dynamic_update_index_in_dim(lefts, record, row_safe, 0)
        return (advance(arriving, blocks_here[row_safe], lower_here[row_safe]), lefts)

    def right_turn(turn, state):
        travel_env, rights = state
        row = turn - (col_count - 1 - column_index)
        active = (row >= 0) & (row < row_count)
        row_safe = jnp.clip(row, 0, row_count - 1)
        arriving = from_behind(travel_env, "col", -1)
        arriving = jnp.where(column_index == col_count - 1, right_edge[row_safe], arriving)
        images = jnp.einsum(
            "kiw,vw->kiv", arriving * live_rows, lower_here[row_safe], precision=HIGHEST
        )
        padded = padded_2(images, (("sec", 0),), 1)
        record = images
        record = jnp.where(active, record, rights[row_safe])
        rights = lax.dynamic_update_index_in_dim(rights, record, row_safe, 0)
        return (retreat(padded, blocks_here[row_safe]), rights)

    lefts_start = jnp.zeros((row_count, sec_local, block_len, bond_width), jnp.float32)
    rights_start = jnp.zeros((row_count, sec_local, block_len, bond_width), jnp.float32)

    def both_turns(turn, state):
        return (left_turn(turn, state[0]), right_turn(turn, state[1]))

    left_state, right_state = lax.fori_loop(
        0, turn_count, both_turns, ((empty_env, lefts_start), (empty_env, rights_start))
    )
    lefts = left_state[1]
    rights = right_state[1]
    padded_all = padded_2(rights, (("sec", 1),), 1)
    shifted_all = jnp.stack(
        [
            padded_all[:, 0:sec_local],
            padded_all[:, 1 : sec_local + 1],
            padded_all[:, 2 : sec_local + 2],
        ],
        axis=1,
    )
    gradient = jnp.einsum("rpkiw,rkjw->rpikj", shifted_all, lefts, precision=HIGHEST) * scale_factor
    return gradient.reshape(row_count, 1, 3, block_len, sec_local * block_len)


def solution(mesh):
    in_specs = (
        P(None, "col", None, None, "sec"),
        P(None, "col", None, None),
        P(None, "sec", None, None),
        P(None, "sec", None, None),
        P("col", "sec"),
    )
    out_specs = P(None, "col", None, None, "sec")
    return jax.shard_map(body, mesh=mesh, in_specs=in_specs, out_specs=out_specs, check_vma=False)
```

profile of v0, /device:TPU:20, one launch (start us, length us, event | category | flops | bytes accessed | tf_op | source)
XLA Modules:
  0.0 224.3 jit_solution(6820923970223870064)
XLA Ops:
  2.2 209.6 %while.21 = (s32[]{:T(128)}, f32[2,64,128]{2,1,0:T(8,128)S(1)}, f32[2,2,64,128]{3,2,1,0:T(8,128)S(1)}, f32[2,64,128]{2,1,0:T(8,128)S(1)}, f32[2,2,64,128]{3,2,1,...) while((s32[]{:T(128)}, f32[2,64,128]{2,1,0:T(8,128)S(1)}, ...), condition=%wide.region_1.2_spmd.clone, body=%wide.region_0.1_spmd.clone.sunk | while | flops 126222592 | bytes 4920369 | solution.py:91
  4.2 4.5 %collective-permute-start.3 = (f32[2,64,128]{2,1,0:T(8,128)S(1)}, f32[2,64,128]{2,1,0:T(8,128)S(1)}, u32[]{:S(2)}, u32[]{:S(2)}) collective-permute-start(f32[2,64,128]{2,1,0:T(8,128)S(1)} %get-tuple-element.476), channel_id=1, source_target_pairs={{4,0},{8,4},{12,8},{16,12},{20,16},{24,20},{28,24},{5,1},{9,5},{13... | collective-permute-start | bytes 196616 | tf_op jit(solution)/shard_map/while/body/eval_jaxpr/ppermute | solution.py:27
  10.9 3.5 %collective-permute-start.4 = (f32[1,64,128]{2,1,0:T(8,128)S(1)}, f32[1,64,128]{2,1,0:T(8,128)S(1)}, u32[]{:S(2)}, u32[]{:S(2)}) collective-permute-start(f32[1,64,128]{2,1,0:T(8,128)S(1)} %get-tuple-element.451), channel_id=1, source_target_pairs={{0,1},{1,2},{2,3},{4,5},{5,6},{6,7},{8,9},{9,10},{10,11},{12,13},{... | collective-permute-start | bytes 98312 | tf_op jit(solution)/shard_map/while/body/eval_jaxpr/ppermute | solution.py:16
  14.4 2.4 %collective-permute-start.5 = (f32[1,64,128]{2,1,0:T(8,128)S(1)}, f32[1,64,128]{2,1,0:T(8,128)S(1)}, u32[]{:S(2)}, u32[]{:S(2)}) collective-permute-start(f32[1,64,128]{2,1,0:T(8,128)S(1)} %get-tuple-element.452), channel_id=1, source_target_pairs={{1,0},{2,1},{3,2},{5,4},{6,5},{7,6},{9,8},{10,9},{11,10},{13,12},{... | collective-permute-start | bytes 98312 | tf_op jit(solution)/shard_map/while/body/eval_jaxpr/ppermute | solution.py:19
  17.1 2.4 %collective-permute-start.1 = (f32[1,2,64,128]{3,2,0,1:T(8,128)S(1)}, f32[1,2,64,128]{3,2,0,1:T(8,128)S(1)}, u32[]{:S(2)}, u32[]{:S(2)}) collective-permute-start(f32[1,2,64,128]{3,2,0,1:T(8,128)S(1)} %get-tuple-element.448), channel_id=1, source_target_pairs={{1,0},{2,1},{3,2},{5,4},{6,5},{7,6},{9,8},{10,9},{11,10},{13,12},{... | collective-permute-start | bytes 196616 | tf_op jit(solution)/shard_map/while/body/eval_jaxpr/ppermute | solution.py:19
  19.5 3.5 %collective-permute-start.2 = (f32[1,2,64,128]{3,2,0,1:T(8,128)S(1)}, f32[1,2,64,128]{3,2,0,1:T(8,128)S(1)}, u32[]{:S(2)}, u32[]{:S(2)}) collective-permute-start(f32[1,2,64,128]{3,2,0,1:T(8,128)S(1)} %get-tuple-element.449), channel_id=1, source_target_pairs={{0,1},{1,2},{2,3},{4,5},{5,6},{6,7},{8,9},{9,10},{10,11},{12,13},{... | collective-permute-start | bytes 196616 | tf_op jit(solution)/shard_map/while/body/eval_jaxpr/ppermute | solution.py:16
  23.6 2.1 collective-permute-done.2
  25.9 1.9 collective-permute-start
  27.8 4.5 %collective-permute-start.3 = (f32[2,64,128]{2,1,0:T(8,128)S(1)}, f32[2,64,128]{2,1,0:T(8,128)S(1)}, u32[]{:S(2)}, u32[]{:S(2)}) collective-permute-start(f32[2,64,128]{2,1,0:T(8,128)S(1)} %get-tuple-element.476), channel_id=1, source_target_pairs={{4,0},{8,4},{12,8},{16,12},{20,16},{24,20},{28,24},{5,1},{9,5},{13... | collective-permute-start | bytes 196616 | tf_op jit(solution)/shard_map/while/body/eval_jaxpr/ppermute | solution.py:27
  34.6 3.5 %collective-permute-start.4 = (f32[1,64,128]{2,1,0:T(8,128)S(1)}, f32[1,64,128]{2,1,0:T(8,128)S(1)}, u32[]{:S(2)}, u32[]{:S(2)}) collective-permute-start(f32[1,64,128]{2,1,0:T(8,128)S(1)} %get-tuple-element.451), channel_id=1, source_target_pairs={{0,1},{1,2},{2,3},{4,5},{5,6},{6,7},{8,9},{9,10},{10,11},{12,13},{... | collective-permute-start | bytes 98312 | tf_op jit(solution)/shard_map/while/body/eval_jaxpr/ppermute | solution.py:16
  38.1 2.4 %collective-permute-start.5 = (f32[1,64,128]{2,1,0:T(8,128)S(1)}, f32[1,64,128]{2,1,0:T(8,128)S(1)}, u32[]{:S(2)}, u32[]{:S(2)}) collective-permute-start(f32[1,64,128]{2,1,0:T(8,128)S(1)} %get-tuple-element.452), channel_id=1, source_target_pairs={{1,0},{2,1},{3,2},{5,4},{6,5},{7,6},{9,8},{10,9},{11,10},{13,12},{... | collective-permute-start | bytes 98312 | tf_op jit(solution)/shard_map/while/body/eval_jaxpr/ppermute | solution.py:19
  40.8 1.9 collective-permute-start.1
  42.7 3.9 %collective-permute-start.2 = (f32[1,2,64,128]{3,2,0,1:T(8,128)S(1)}, f32[1,2,64,128]{3,2,0,1:T(8,128)S(1)}, u32[]{:S(2)}, u32[]{:S(2)}) collective-permute-start(f32[1,2,64,128]{3,2,0,1:T(8,128)S(1)} %get-tuple-element.449), channel_id=1, source_target_pairs={{0,1},{1,2},{2,3},{4,5},{5,6},{6,7},{8,9},{9,10},{10,11},{12,13},{... | collective-permute-start | bytes 196616 | tf_op jit(solution)/shard_map/while/body/eval_jaxpr/ppermute | solution.py:16
  51.1 4.5 %collective-permute-start.3 = (f32[2,64,128]{2,1,0:T(8,128)S(1)}, f32[2,64,128]{2,1,0:T(8,128)S(1)}, u32[]{:S(2)}, u32[]{:S(2)}) collective-permute-start(f32[2,64,128]{2,1,0:T(8,128)S(1)} %get-tuple-element.476), channel_id=1, source_target_pairs={{4,0},{8,4},{12,8},{16,12},{20,16},{24,20},{28,24},{5,1},{9,5},{13... | collective-permute-start | bytes 196616 | tf_op jit(solution)/shard_map/while/body/eval_jaxpr/ppermute | solution.py:27
  57.8 3.9 %collective-permute-start.4 = (f32[1,64,128]{2,1,0:T(8,128)S(1)}, f32[1,64,128]{2,1,0:T(8,128)S(1)}, u32[]{:S(2)}, u32[]{:S(2)}) collective-permute-start(f32[1,64,128]{2,1,0:T(8,128)S(1)} %get-tuple-element.451), channel_id=1, source_target_pairs={{0,1},{1,2},{2,3},{4,5},{5,6},{6,7},{8,9},{9,10},{10,11},{12,13},{... | collective-permute-start | bytes 98312 | tf_op jit(solution)/shard_map/while/body/eval_jaxpr/ppermute | solution.py:16
  61.8 1.9 collective-permute-start.5
  64.1 1.9 collective-permute-start.1
  66.0 3.9 %collective-permute-start.2 = (f32[1,2,64,128]{3,2,0,1:T(8,128)S(1)}, f32[1,2,64,128]{3,2,0,1:T(8,128)S(1)}, u32[]{:S(2)}, u32[]{:S(2)}) collective-permute-start(f32[1,2,64,128]{3,2,0,1:T(8,128)S(1)} %get-tuple-element.449), channel_id=1, source_target_pairs={{0,1},{1,2},{2,3},{4,5},{5,6},{6,7},{8,9},{9,10},{10,11},{12,13},{... | collective-permute-start | bytes 196616 | tf_op jit(solution)/shard_map/while/body/eval_jaxpr/ppermute | solution.py:16
  74.3 4.5 %collective-permute-start.3 = (f32[2,64,128]{2,1,0:T(8,128)S(1)}, f32[2,64,128]{2,1,0:T(8,128)S(1)}, u32[]{:S(2)}, u32[]{:S(2)}) collective-permute-start(f32[2,64,128]{2,1,0:T(8,128)S(1)} %get-tuple-element.476), channel_id=1, source_target_pairs={{4,0},{8,4},{12,8},{16,12},{20,16},{24,20},{28,24},{5,1},{9,5},{13... | collective-permute-start | bytes 196616 | tf_op jit(solution)/shard_map/while/body/eval_jaxpr/ppermute | solution.py:27
  81.1 3.9 %collective-permute-start.4 = (f32[1,64,128]{2,1,0:T(8,128)S(1)}, f32[1,64,128]{2,1,0:T(8,128)S(1)}, u32[]{:S(2)}, u32[]{:S(2)}) collective-permute-start(f32[1,64,128]{2,1,0:T(8,128)S(1)} %get-tuple-element.451), channel_id=1, source_target_pairs={{0,1},{1,2},{2,3},{4,5},{5,6},{6,7},{8,9},{9,10},{10,11},{12,13},{... | collective-permute-start | bytes 98312 | tf_op jit(solution)/shard_map/while/body/eval_jaxpr/ppermute | solution.py:16
  85.0 1.9 collective-permute-start.5
  87.3 1.9 collective-permute-start.1
  89.2 3.9 %collective-permute-start.2 = (f32[1,2,64,128]{3,2,0,1:T(8,128)S(1)}, f32[1,2,64,128]{3,2,0,1:T(8,128)S(1)}, u32[]{:S(2)}, u32[]{:S(2)}) collective-permute-start(f32[1,2,64,128]{3,2,0,1:T(8,128)S(1)} %get-tuple-element.449), channel_id=1, source_target_pairs={{0,1},{1,2},{2,3},{4,5},{5,6},{6,7},{8,9},{9,10},{10,11},{12,13},{... | collective-permute-start | bytes 196616 | tf_op jit(solution)/shard_map/while/body/eval_jaxpr/ppermute | solution.py:16
  97.6 4.5 %collective-permute-start.3 = (f32[2,64,128]{2,1,0:T(8,128)S(1)}, f32[2,64,128]{2,1,0:T(8,128)S(1)}, u32[]{:S(2)}, u32[]{:S(2)}) collective-permute-start(f32[2,64,128]{2,1,0:T(8,128)S(1)} %get-tuple-element.476), channel_id=1, source_target_pairs={{4,0},{8,4},{12,8},{16,12},{20,16},{24,20},{28,24},{5,1},{9,5},{13... | collective-permute-start | bytes 196616 | tf_op jit(solution)/shard_map/while/body/eval_jaxpr/ppermute | solution.py:27
  104.3 3.9 %collective-permute-start.4 = (f32[1,64,128]{2,1,0:T(8,128)S(1)}, f32[1,64,128]{2,1,0:T(8,128)S(1)}, u32[]{:S(2)}, u32[]{:S(2)}) collective-permute-start(f32[1,64,128]{2,1,0:T(8,128)S(1)} %get-tuple-element.451), channel_id=1, source_target_pairs={{0,1},{1,2},{2,3},{4,5},{5,6},{6,7},{8,9},{9,10},{10,11},{12,13},{... | collective-permute-start | bytes 98312 | tf_op jit(solution)/shard_map/while/body/eval_jaxpr/ppermute | solution.py:16
  108.2 1.9 collective-permute-start.5
  112.5 3.9 %collective-permute-start.2 = (f32[1,2,64,128]{3,2,0,1:T(8,128)S(1)}, f32[1,2,64,128]{3,2,0,1:T(8,128)S(1)}, u32[]{:S(2)}, u32[]{:S(2)}) collective-permute-start(f32[1,2,64,128]{3,2,0,1:T(8,128)S(1)} %get-tuple-element.449), channel_id=1, source_target_pairs={{0,1},{1,2},{2,3},{4,5},{5,6},{6,7},{8,9},{9,10},{10,11},{12,13},{... | collective-permute-start | bytes 196616 | tf_op jit(solution)/shard_map/while/body/eval_jaxpr/ppermute | solution.py:16
  120.8 4.5 %collective-permute-start.3 = (f32[2,64,128]{2,1,0:T(8,128)S(1)}, f32[2,64,128]{2,1,0:T(8,128)S(1)}, u32[]{:S(2)}, u32[]{:S(2)}) collective-permute-start(f32[2,64,128]{2,1,0:T(8,128)S(1)} %get-tuple-element.476), channel_id=1, source_target_pairs={{4,0},{8,4},{12,8},{16,12},{20,16},{24,20},{28,24},{5,1},{9,5},{13... | collective-permute-start | bytes 196616 | tf_op jit(solution)/shard_map/while/body/eval_jaxpr/ppermute | solution.py:27
  127.6 3.9 %collective-permute-start.4 = (f32[1,64,128]{2,1,0:T(8,128)S(1)}, f32[1,64,128]{2,1,0:T(8,128)S(1)}, u32[]{:S(2)}, u32[]{:S(2)}) collective-permute-start(f32[1,64,128]{2,1,0:T(8,128)S(1)} %get-tuple-element.451), channel_id=1, source_target_pairs={{0,1},{1,2},{2,3},{4,5},{5,6},{6,7},{8,9},{9,10},{10,11},{12,13},{... | collective-permute-start | bytes 98312 | tf_op jit(solution)/shard_map/while/body/eval_jaxpr/ppermute | solution.py:16
  131.5 1.9 collective-permute-start.5
  133.8 1.9 collective-permute-start.1
  135.7 3.9 %collective-permute-start.2 = (f32[1,2,64,128]{3,2,0,1:T(8,128)S(1)}, f32[1,2,64,128]{3,2,0,1:T(8,128)S(1)}, u32[]{:S(2)}, u32[]{:S(2)}) collective-permute-start(f32[1,2,64,128]{3,2,0,1:T(8,128)S(1)} %get-tuple-element.449), channel_id=1, source_target_pairs={{0,1},{1,2},{2,3},{4,5},{5,6},{6,7},{8,9},{9,10},{10,11},{12,13},{... | collective-permute-start | bytes 196616 | tf_op jit(solution)/shard_map/while/body/eval_jaxpr/ppermute | solution.py:16
  142.1 1.9 collective-permute-start
  144.1 4.5 %collective-permute-start.3 = (f32[2,64,128]{2,1,0:T(8,128)S(1)}, f32[2,64,128]{2,1,0:T(8,128)S(1)}, u32[]{:S(2)}, u32[]{:S(2)}) collective-permute-start(f32[2,64,128]{2,1,0:T(8,128)S(1)} %get-tuple-element.476), channel_id=1, source_target_pairs={{4,0},{8,4},{12,8},{16,12},{20,16},{24,20},{28,24},{5,1},{9,5},{13... | collective-permute-start | bytes 196616 | tf_op jit(solution)/shard_map/while/body/eval_jaxpr/ppermute | solution.py:27
  150.8 3.9 %collective-permute-start.4 = (f32[1,64,128]{2,1,0:T(8,128)S(1)}, f32[1,64,128]{2,1,0:T(8,128)S(1)}, u32[]{:S(2)}, u32[]{:S(2)}) collective-permute-start(f32[1,64,128]{2,1,0:T(8,128)S(1)} %get-tuple-element.451), channel_id=1, source_target_pairs={{0,1},{1,2},{2,3},{4,5},{5,6},{6,7},{8,9},{9,10},{10,11},{12,13},{... | collective-permute-start | bytes 98312 | tf_op jit(solution)/shard_map/while/body/eval_jaxpr/ppermute | solution.py:16
  154.7 1.9 collective-permute-start.5
  157.0 1.9 collective-permute-start.1
  159.0 3.9 %collective-permute-start.2 = (f32[1,2,64,128]{3,2,0,1:T(8,128)S(1)}, f32[1,2,64,128]{3,2,0,1:T(8,128)S(1)}, u32[]{:S(2)}, u32[]{:S(2)}) collective-permute-start(f32[1,2,64,128]{3,2,0,1:T(8,128)S(1)} %get-tuple-element.449), channel_id=1, source_target_pairs={{0,1},{1,2},{2,3},{4,5},{5,6},{6,7},{8,9},{9,10},{10,11},{12,13},{... | collective-permute-start | bytes 196616 | tf_op jit(solution)/shard_map/while/body/eval_jaxpr/ppermute | solution.py:16
  165.4 1.9 collective-permute-start
  167.3 4.5 %collective-permute-start.3 = (f32[2,64,128]{2,1,0:T(8,128)S(1)}, f32[2,64,128]{2,1,0:T(8,128)S(1)}, u32[]{:S(2)}, u32[]{:S(2)}) collective-permute-start(f32[2,64,128]{2,1,0:T(8,128)S(1)} %get-tuple-element.476), channel_id=1, source_target_pairs={{4,0},{8,4},{12,8},{16,12},{20,16},{24,20},{28,24},{5,1},{9,5},{13... | collective-permute-start | bytes 196616 | tf_op jit(solution)/shard_map/while/body/eval_jaxpr/ppermute | solution.py:27
  174.0 3.9 %collective-permute-start.4 = (f32[1,64,128]{2,1,0:T(8,128)S(1)}, f32[1,64,128]{2,1,0:T(8,128)S(1)}, u32[]{:S(2)}, u32[]{:S(2)}) collective-permute-start(f32[1,64,128]{2,1,0:T(8,128)S(1)} %get-tuple-element.451), channel_id=1, source_target_pairs={{0,1},{1,2},{2,3},{4,5},{5,6},{6,7},{8,9},{9,10},{10,11},{12,13},{... | collective-permute-start | bytes 98312 | tf_op jit(solution)/shard_map/while/body/eval_jaxpr/ppermute | solution.py:16
  182.2 3.9 %collective-permute-start.2 = (f32[1,2,64,128]{3,2,0,1:T(8,128)S(1)}, f32[1,2,64,128]{3,2,0,1:T(8,128)S(1)}, u32[]{:S(2)}, u32[]{:S(2)}) collective-permute-start(f32[1,2,64,128]{3,2,0,1:T(8,128)S(1)} %get-tuple-element.449), channel_id=1, source_target_pairs={{0,1},{1,2},{2,3},{4,5},{5,6},{6,7},{8,9},{9,10},{10,11},{12,13},{... | collective-permute-start | bytes 196616 | tf_op jit(solution)/shard_map/while/body/eval_jaxpr/ppermute | solution.py:16
  190.5 4.5 %collective-permute-start.3 = (f32[2,64,128]{2,1,0:T(8,128)S(1)}, f32[2,64,128]{2,1,0:T(8,128)S(1)}, u32[]{:S(2)}, u32[]{:S(2)}) collective-permute-start(f32[2,64,128]{2,1,0:T(8,128)S(1)} %get-tuple-element.476), channel_id=1, source_target_pairs={{4,0},{8,4},{12,8},{16,12},{20,16},{24,20},{28,24},{5,1},{9,5},{13... | collective-permute-start | bytes 196616 | tf_op jit(solution)/shard_map/while/body/eval_jaxpr/ppermute | solution.py:27
  197.3 3.9 %collective-permute-start.4 = (f32[1,64,128]{2,1,0:T(8,128)S(1)}, f32[1,64,128]{2,1,0:T(8,128)S(1)}, u32[]{:S(2)}, u32[]{:S(2)}) collective-permute-start(f32[1,64,128]{2,1,0:T(8,128)S(1)} %get-tuple-element.451), channel_id=1, source_target_pairs={{0,1},{1,2},{2,3},{4,5},{5,6},{6,7},{8,9},{9,10},{10,11},{12,13},{... | collective-permute-start | bytes 98312 | tf_op jit(solution)/shard_map/while/body/eval_jaxpr/ppermute | solution.py:16
  205.4 3.9 %collective-permute-start.2 = (f32[1,2,64,128]{3,2,0,1:T(8,128)S(1)}, f32[1,2,64,128]{3,2,0,1:T(8,128)S(1)}, u32[]{:S(2)}, u32[]{:S(2)}) collective-permute-start(f32[1,2,64,128]{3,2,0,1:T(8,128)S(1)} %get-tuple-element.449), channel_id=1, source_target_pairs={{0,1},{1,2},{2,3},{4,5},{5,6},{6,7},{8,9},{9,10},{10,11},{12,13},{... | collective-permute-start | bytes 196616 | tf_op jit(solution)/shard_map/while/body/eval_jaxpr/ppermute | solution.py:16
  211.9 4.1 %collective-permute-start.6 = (f32[2,1,64,128]{3,2,1,0:T(8,128)S(1)}, f32[2,1,64,128]{3,2,1,0:T(8,128)S(1)}, u32[]{:S(2)}, u32[]{:S(2)}) collective-permute-start(f32[2,1,64,128]{3,2,1,0:T(8,128)S(1)} %get-tuple-element.349), channel_id=1, source_target_pairs={{0,1},{1,2},{2,3},{4,5},{5,6},{6,7},{8,9},{9,10},{10,11},{12,13},{... | collective-permute-start | bytes 196616 | tf_op jit(solution)/shard_map/ppermute | solution.py:16
  215.9 1.9 collective-permute-start.7
  218.0 4.1 %collective-permute-done.7 = f32[2,1,64,128]{3,2,1,0:T(8,128)S(1)} collective-permute-done((f32[2,1,64,128]{3,2,1,0:T(8,128)S(1)}, f32[2,1,64,128]{3,2,1,0:T(8,128)S(1)}, u32[]{:S(2)}, u32[]{:S(2)}) %collective-permute-start.7) | collective-permute-done | bytes 65568 | tf_op jit(solution)/shard_map/ppermute | solution.py:19
  (210 shorter events, 68.0 us)
Async XLA Ops:
  2.2 14.5 %collective-permute-start = (f32[2,64,128]{2,1,0:T(8,128)S(1)}, f32[2,64,128]{2,1,0:T(8,128)S(1)}, u32[]{:S(2)}, u32[]{:S(2)}) collective-permute-start(f32[2,64,128]{2,1,0:T(8,128)S(1)} %broadcast_select_fusion.2), channel_id=1, source_target_pairs={{0,4},{4,8},{8,12},{12,16},{16,20},{20,24},{24,28},{1,5},{5,9},{9,... | collective-permute-start | bytes 196616 | tf_op jit(solution)/shard_map/while/body/eval_jaxpr/ppermute | solution.py:27
  4.2 6.4 %collective-permute-start.3 = (f32[2,64,128]{2,1,0:T(8,128)S(1)}, f32[2,64,128]{2,1,0:T(8,128)S(1)}, u32[]{:S(2)}, u32[]{:S(2)}) collective-permute-start(f32[2,64,128]{2,1,0:T(8,128)S(1)} %get-tuple-element.476), channel_id=1, source_target_pairs={{4,0},{8,4},{12,8},{16,12},{20,16},{24,20},{28,24},{5,1},{9,5},{13... | collective-permute-start | bytes 196616 | tf_op jit(solution)/shard_map/while/body/eval_jaxpr/ppermute | solution.py:27
  10.9 12.1 %collective-permute-start.4 = (f32[1,64,128]{2,1,0:T(8,128)S(1)}, f32[1,64,128]{2,1,0:T(8,128)S(1)}, u32[]{:S(2)}, u32[]{:S(2)}) collective-permute-start(f32[1,64,128]{2,1,0:T(8,128)S(1)} %get-tuple-element.451), channel_id=1, source_target_pairs={{0,1},{1,2},{2,3},{4,5},{5,6},{6,7},{8,9},{9,10},{10,11},{12,13},{... | collective-permute-start | bytes 98312 | tf_op jit(solution)/shard_map/while/body/eval_jaxpr/ppermute | solution.py:16
  14.4 8.6 %collective-permute-start.5 = (f32[1,64,128]{2,1,0:T(8,128)S(1)}, f32[1,64,128]{2,1,0:T(8,128)S(1)}, u32[]{:S(2)}, u32[]{:S(2)}) collective-permute-start(f32[1,64,128]{2,1,0:T(8,128)S(1)} %get-tuple-element.452), channel_id=1, source_target_pairs={{1,0},{2,1},{3,2},{5,4},{6,5},{7,6},{9,8},{10,9},{11,10},{13,12},{... | collective-permute-start | bytes 98312 | tf_op jit(solution)/shard_map/while/body/eval_jaxpr/ppermute | solution.py:19
  17.1 6.5 %collective-permute-start.1 = (f32[1,2,64,128]{3,2,0,1:T(8,128)S(1)}, f32[1,2,64,128]{3,2,0,1:T(8,128)S(1)}, u32[]{:S(2)}, u32[]{:S(2)}) collective-permute-start(f32[1,2,64,128]{3,2,0,1:T(8,128)S(1)} %get-tuple-element.448), channel_id=1, source_target_pairs={{1,0},{2,1},{3,2},{5,4},{6,5},{7,6},{9,8},{10,9},{11,10},{13,12},{... | collective-permute-start | bytes 196616 | tf_op jit(solution)/shard_map/while/body/eval_jaxpr/ppermute | solution.py:19
  19.5 6.2 %collective-permute-start.2 = (f32[1,2,64,128]{3,2,0,1:T(8,128)S(1)}, f32[1,2,64,128]{3,2,0,1:T(8,128)S(1)}, u32[]{:S(2)}, u32[]{:S(2)}) collective-permute-start(f32[1,2,64,128]{3,2,0,1:T(8,128)S(1)} %get-tuple-element.449), channel_id=1, source_target_pairs={{0,1},{1,2},{2,3},{4,5},{5,6},{6,7},{8,9},{9,10},{10,11},{12,13},{... | collective-permute-start | bytes 196616 | tf_op jit(solution)/shard_map/while/body/eval_jaxpr/ppermute | solution.py:16
  25.9 14.5 %collective-permute-start = (f32[2,64,128]{2,1,0:T(8,128)S(1)}, f32[2,64,128]{2,1,0:T(8,128)S(1)}, u32[]{:S(2)}, u32[]{:S(2)}) collective-permute-start(f32[2,64,128]{2,1,0:T(8,128)S(1)} %broadcast_select_fusion.2), channel_id=1, source_target_pairs={{0,4},{4,8},{8,12},{12,16},{16,20},{20,24},{24,28},{1,5},{5,9},{9,... | collective-permute-start | bytes 196616 | tf_op jit(solution)/shard_map/while/body/eval_jaxpr/ppermute | solution.py:27
  27.8 6.4 %collective-permute-start.3 = (f32[2,64,128]{2,1,0:T(8,128)S(1)}, f32[2,64,128]{2,1,0:T(8,128)S(1)}, u32[]{:S(2)}, u32[]{:S(2)}) collective-permute-start(f32[2,64,128]{2,1,0:T(8,128)S(1)} %get-tuple-element.476), channel_id=1, source_target_pairs={{4,0},{8,4},{12,8},{16,12},{20,16},{24,20},{28,24},{5,1},{9,5},{13... | collective-permute-start | bytes 196616 | tf_op jit(solution)/shard_map/while/body/eval_jaxpr/ppermute | solution.py:27
  34.6 12.1 %collective-permute-start.4 = (f32[1,64,128]{2,1,0:T(8,128)S(1)}, f32[1,64,128]{2,1,0:T(8,128)S(1)}, u32[]{:S(2)}, u32[]{:S(2)}) collective-permute-start(f32[1,64,128]{2,1,0:T(8,128)S(1)} %get-tuple-element.451), channel_id=1, source_target_pairs={{0,1},{1,2},{2,3},{4,5},{5,6},{6,7},{8,9},{9,10},{10,11},{12,13},{... | collective-permute-start | bytes 98312 | tf_op jit(solution)/shard_map/while/body/eval_jaxpr/ppermute | solution.py:16
  38.1 8.6 %collective-permute-start.5 = (f32[1,64,128]{2,1,0:T(8,128)S(1)}, f32[1,64,128]{2,1,0:T(8,128)S(1)}, u32[]{:S(2)}, u32[]{:S(2)}) collective-permute-start(f32[1,64,128]{2,1,0:T(8,128)S(1)} %get-tuple-element.452), channel_id=1, source_target_pairs={{1,0},{2,1},{3,2},{5,4},{6,5},{7,6},{9,8},{10,9},{11,10},{13,12},{... | collective-permute-start | bytes 98312 | tf_op jit(solution)/shard_map/while/body/eval_jaxpr/ppermute | solution.py:19
  40.8 6.5 %collective-permute-start.1 = (f32[1,2,64,128]{3,2,0,1:T(8,128)S(1)}, f32[1,2,64,128]{3,2,0,1:T(8,128)S(1)}, u32[]{:S(2)}, u32[]{:S(2)}) collective-permute-start(f32[1,2,64,128]{3,2,0,1:T(8,128)S(1)} %get-tuple-element.448), channel_id=1, source_target_pairs={{1,0},{2,1},{3,2},{5,4},{6,5},{7,6},{9,8},{10,9},{11,10},{13,12},{... | collective-permute-start | bytes 196616 | tf_op jit(solution)/shard_map/while/body/eval_jaxpr/ppermute | solution.py:19
  42.7 6.2 %collective-permute-start.2 = (f32[1,2,64,128]{3,2,0,1:T(8,128)S(1)}, f32[1,2,64,128]{3,2,0,1:T(8,128)S(1)}, u32[]{:S(2)}, u32[]{:S(2)}) collective-permute-start(f32[1,2,64,128]{3,2,0,1:T(8,128)S(1)} %get-tuple-element.449), channel_id=1, source_target_pairs={{0,1},{1,2},{2,3},{4,5},{5,6},{6,7},{8,9},{9,10},{10,11},{12,13},{... | collective-permute-start | bytes 196616 | tf_op jit(solution)/shard_map/while/body/eval_jaxpr/ppermute | solution.py:16
  49.2 14.5 %collective-permute-start = (f32[2,64,128]{2,1,0:T(8,128)S(1)}, f32[2,64,128]{2,1,0:T(8,128)S(1)}, u32[]{:S(2)}, u32[]{:S(2)}) collective-permute-start(f32[2,64,128]{2,1,0:T(8,128)S(1)} %broadcast_select_fusion.2), channel_id=1, source_target_pairs={{0,4},{4,8},{8,12},{12,16},{16,20},{20,24},{24,28},{1,5},{5,9},{9,... | collective-permute-start | bytes 196616 | tf_op jit(solution)/shard_map/while/body/eval_jaxpr/ppermute | solution.py:27
  51.1 6.4 %collective-permute-start.3 = (f32[2,64,128]{2,1,0:T(8,128)S(1)}, f32[2,64,128]{2,1,0:T(8,128)S(1)}, u32[]{:S(2)}, u32[]{:S(2)}) collective-permute-start(f32[2,64,128]{2,1,0:T(8,128)S(1)} %get-tuple-element.476), channel_id=1, source_target_pairs={{4,0},{8,4},{12,8},{16,12},{20,16},{24,20},{28,24},{5,1},{9,5},{13... | collective-permute-start | bytes 196616 | tf_op jit(solution)/shard_map/while/body/eval_jaxpr/ppermute | solution.py:27
  57.8 12.1 %collective-permute-start.4 = (f32[1,64,128]{2,1,0:T(8,128)S(1)}, f32[1,64,128]{2,1,0:T(8,128)S(1)}, u32[]{:S(2)}, u32[]{:S(2)}) collective-permute-start(f32[1,64,128]{2,1,0:T(8,128)S(1)} %get-tuple-element.451), channel_id=1, source_target_pairs={{0,1},{1,2},{2,3},{4,5},{5,6},{6,7},{8,9},{9,10},{10,11},{12,13},{... | collective-permute-start | bytes 98312 | tf_op jit(solution)/shard_map/while/body/eval_jaxpr/ppermute | solution.py:16
  61.8 8.2 %collective-permute-start.5 = (f32[1,64,128]{2,1,0:T(8,128)S(1)}, f32[1,64,128]{2,1,0:T(8,128)S(1)}, u32[]{:S(2)}, u32[]{:S(2)}) collective-permute-start(f32[1,64,128]{2,1,0:T(8,128)S(1)} %get-tuple-element.452), channel_id=1, source_target_pairs={{1,0},{2,1},{3,2},{5,4},{6,5},{7,6},{9,8},{10,9},{11,10},{13,12},{... | collective-permute-start | bytes 98312 | tf_op jit(solution)/shard_map/while/body/eval_jaxpr/ppermute | solution.py:19
  64.1 6.5 %collective-permute-start.1 = (f32[1,2,64,128]{3,2,0,1:T(8,128)S(1)}, f32[1,2,64,128]{3,2,0,1:T(8,128)S(1)}, u32[]{:S(2)}, u32[]{:S(2)}) collective-permute-start(f32[1,2,64,128]{3,2,0,1:T(8,128)S(1)} %get-tuple-element.448), channel_id=1, source_target_pairs={{1,0},{2,1},{3,2},{5,4},{6,5},{7,6},{9,8},{10,9},{11,10},{13,12},{... | collective-permute-start | bytes 196616 | tf_op jit(solution)/shard_map/while/body/eval_jaxpr/ppermute | solution.py:19
  66.0 6.2 %collective-permute-start.2 = (f32[1,2,64,128]{3,2,0,1:T(8,128)S(1)}, f32[1,2,64,128]{3,2,0,1:T(8,128)S(1)}, u32[]{:S(2)}, u32[]{:S(2)}) collective-permute-start(f32[1,2,64,128]{3,2,0,1:T(8,128)S(1)} %get-tuple-element.449), channel_id=1, source_target_pairs={{0,1},{1,2},{2,3},{4,5},{5,6},{6,7},{8,9},{9,10},{10,11},{12,13},{... | collective-permute-start | bytes 196616 | tf_op jit(solution)/shard_map/while/body/eval_jaxpr/ppermute | solution.py:16
  72.4 14.5 %collective-permute-start = (f32[2,64,128]{2,1,0:T(8,128)S(1)}, f32[2,64,128]{2,1,0:T(8,128)S(1)}, u32[]{:S(2)}, u32[]{:S(2)}) collective-permute-start(f32[2,64,128]{2,1,0:T(8,128)S(1)} %broadcast_select_fusion.2), channel_id=1, source_target_pairs={{0,4},{4,8},{8,12},{12,16},{16,20},{20,24},{24,28},{1,5},{5,9},{9,... | collective-permute-start | bytes 196616 | tf_op jit(solution)/shard_map/while/body/eval_jaxpr/ppermute | solution.py:27
  74.3 6.4 %collective-permute-start.3 = (f32[2,64,128]{2,1,0:T(8,128)S(1)}, f32[2,64,128]{2,1,0:T(8,128)S(1)}, u32[]{:S(2)}, u32[]{:S(2)}) collective-permute-start(f32[2,64,128]{2,1,0:T(8,128)S(1)} %get-tuple-element.476), channel_id=1, source_target_pairs={{4,0},{8,4},{12,8},{16,12},{20,16},{24,20},{28,24},{5,1},{9,5},{13... | collective-permute-start | bytes 196616 | tf_op jit(solution)/shard_map/while/body/eval_jaxpr/ppermute | solution.py:27
  81.1 12.1 %collective-permute-start.4 = (f32[1,64,128]{2,1,0:T(8,128)S(1)}, f32[1,64,128]{2,1,0:T(8,128)S(1)}, u32[]{:S(2)}, u32[]{:S(2)}) collective-permute-start(f32[1,64,128]{2,1,0:T(8,128)S(1)} %get-tuple-element.451), channel_id=1, source_target_pairs={{0,1},{1,2},{2,3},{4,5},{5,6},{6,7},{8,9},{9,10},{10,11},{12,13},{... | collective-permute-start | bytes 98312 | tf_op jit(solution)/shard_map/while/body/eval_jaxpr/ppermute | solution.py:16
  85.0 8.2 %collective-permute-start.5 = (f32[1,64,128]{2,1,0:T(8,128)S(1)}, f32[1,64,128]{2,1,0:T(8,128)S(1)}, u32[]{:S(2)}, u32[]{:S(2)}) collective-permute-start(f32[1,64,128]{2,1,0:T(8,128)S(1)} %get-tuple-element.452), channel_id=1, source_target_pairs={{1,0},{2,1},{3,2},{5,4},{6,5},{7,6},{9,8},{10,9},{11,10},{13,12},{... | collective-permute-start | bytes 98312 | tf_op jit(solution)/shard_map/while/body/eval_jaxpr/ppermute | solution.py:19
  87.3 6.5 %collective-permute-start.1 = (f32[1,2,64,128]{3,2,0,1:T(8,128)S(1)}, f32[1,2,64,128]{3,2,0,1:T(8,128)S(1)}, u32[]{:S(2)}, u32[]{:S(2)}) collective-permute-start(f32[1,2,64,128]{3,2,0,1:T(8,128)S(1)} %get-tuple-element.448), channel_id=1, source_target_pairs={{1,0},{2,1},{3,2},{5,4},{6,5},{7,6},{9,8},{10,9},{11,10},{13,12},{... | collective-permute-start | bytes 196616 | tf_op jit(solution)/shard_map/while/body/eval_jaxpr/ppermute | solution.py:19
  95.6 14.5 %collective-permute-start = (f32[2,64,128]{2,1,0:T(8,128)S(1)}, f32[2,64,128]{2,1,0:T(8,128)S(1)}, u32[]{:S(2)}, u32[]{:S(2)}) collective-permute-start(f32[2,64,128]{2,1,0:T(8,128)S(1)} %broadcast_select_fusion.2), channel_id=1, source_target_pairs={{0,4},{4,8},{8,12},{12,16},{16,20},{20,24},{24,28},{1,5},{5,9},{9,... | collective-permute-start | bytes 196616 | tf_op jit(solution)/shard_map/while/body/eval_jaxpr/ppermute | solution.py:27
  97.6 6.4 %collective-permute-start.3 = (f32[2,64,128]{2,1,0:T(8,128)S(1)}, f32[2,64,128]{2,1,0:T(8,128)S(1)}, u32[]{:S(2)}, u32[]{:S(2)}) collective-permute-start(f32[2,64,128]{2,1,0:T(8,128)S(1)} %get-tuple-element.476), channel_id=1, source_target_pairs={{4,0},{8,4},{12,8},{16,12},{20,16},{24,20},{28,24},{5,1},{9,5},{13... | collective-permute-start | bytes 196616 | tf_op jit(solution)/shard_map/while/body/eval_jaxpr/ppermute | solution.py:27
  104.3 12.1 %collective-permute-start.4 = (f32[1,64,128]{2,1,0:T(8,128)S(1)}, f32[1,64,128]{2,1,0:T(8,128)S(1)}, u32[]{:S(2)}, u32[]{:S(2)}) collective-permute-start(f32[1,64,128]{2,1,0:T(8,128)S(1)} %get-tuple-element.451), channel_id=1, source_target_pairs={{0,1},{1,2},{2,3},{4,5},{5,6},{6,7},{8,9},{9,10},{10,11},{12,13},{... | collective-permute-start | bytes 98312 | tf_op jit(solution)/shard_map/while/body/eval_jaxpr/ppermute | solution.py:16
  108.2 8.2 %collective-permute-start.5 = (f32[1,64,128]{2,1,0:T(8,128)S(1)}, f32[1,64,128]{2,1,0:T(8,128)S(1)}, u32[]{:S(2)}, u32[]{:S(2)}) collective-permute-start(f32[1,64,128]{2,1,0:T(8,128)S(1)} %get-tuple-element.452), channel_id=1, source_target_pairs={{1,0},{2,1},{3,2},{5,4},{6,5},{7,6},{9,8},{10,9},{11,10},{13,12},{... | collective-permute-start | bytes 98312 | tf_op jit(solution)/shard_map/while/body/eval_jaxpr/ppermute | solution.py:19
  110.5 6.5 %collective-permute-start.1 = (f32[1,2,64,128]{3,2,0,1:T(8,128)S(1)}, f32[1,2,64,128]{3,2,0,1:T(8,128)S(1)}, u32[]{:S(2)}, u32[]{:S(2)}) collective-permute-start(f32[1,2,64,128]{3,2,0,1:T(8,128)S(1)} %get-tuple-element.448), channel_id=1, source_target_pairs={{1,0},{2,1},{3,2},{5,4},{6,5},{7,6},{9,8},{10,9},{11,10},{13,12},{... | collective-permute-start | bytes 196616 | tf_op jit(solution)/shard_map/while/body/eval_jaxpr/ppermute | solution.py:19
  118.9 14.5 %collective-permute-start = (f32[2,64,128]{2,1,0:T(8,128)S(1)}, f32[2,64,128]{2,1,0:T(8,128)S(1)}, u32[]{:S(2)}, u32[]{:S(2)}) collective-permute-start(f32[2,64,128]{2,1,0:T(8,128)S(1)} %broadcast_select_fusion.2), channel_id=1, source_target_pairs={{0,4},{4,8},{8,12},{12,16},{16,20},{20,24},{24,28},{1,5},{5,9},{9,... | collective-permute-start | bytes 196616 | tf_op jit(solution)/shard_map/while/body/eval_jaxpr/ppermute | solution.py:27
  120.8 6.4 %collective-permute-start.3 = (f32[2,64,128]{2,1,0:T(8,128)S(1)}, f32[2,64,128]{2,1,0:T(8,128)S(1)}, u32[]{:S(2)}, u32[]{:S(2)}) collective-permute-start(f32[2,64,128]{2,1,0:T(8,128)S(1)} %get-tuple-element.476), channel_id=1, source_target_pairs={{4,0},{8,4},{12,8},{16,12},{20,16},{24,20},{28,24},{5,1},{9,5},{13... | collective-permute-start | bytes 196616 | tf_op jit(solution)/shard_map/while/body/eval_jaxpr/ppermute | solution.py:27
  127.6 12.1 %collective-permute-start.4 = (f32[1,64,128]{2,1,0:T(8,128)S(1)}, f32[1,64,128]{2,1,0:T(8,128)S(1)}, u32[]{:S(2)}, u32[]{:S(2)}) collective-permute-start(f32[1,64,128]{2,1,0:T(8,128)S(1)} %get-tuple-element.451), channel_id=1, source_target_pairs={{0,1},{1,2},{2,3},{4,5},{5,6},{6,7},{8,9},{9,10},{10,11},{12,13},{... | collective-permute-start | bytes 98312 | tf_op jit(solution)/shard_map/while/body/eval_jaxpr/ppermute | solution.py:16
  131.5 8.2 %collective-permute-start.5 = (f32[1,64,128]{2,1,0:T(8,128)S(1)}, f32[1,64,128]{2,1,0:T(8,128)S(1)}, u32[]{:S(2)}, u32[]{:S(2)}) collective-permute-start(f32[1,64,128]{2,1,0:T(8,128)S(1)} %get-tuple-element.452), channel_id=1, source_target_pairs={{1,0},{2,1},{3,2},{5,4},{6,5},{7,6},{9,8},{10,9},{11,10},{13,12},{... | collective-permute-start | bytes 98312 | tf_op jit(solution)/shard_map/while/body/eval_jaxpr/ppermute | solution.py:19
  133.8 6.5 %collective-permute-start.1 = (f32[1,2,64,128]{3,2,0,1:T(8,128)S(1)}, f32[1,2,64,128]{3,2,0,1:T(8,128)S(1)}, u32[]{:S(2)}, u32[]{:S(2)}) collective-permute-start(f32[1,2,64,128]{3,2,0,1:T(8,128)S(1)} %get-tuple-element.448), channel_id=1, source_target_pairs={{1,0},{2,1},{3,2},{5,4},{6,5},{7,6},{9,8},{10,9},{11,10},{13,12},{... | collective-permute-start | bytes 196616 | tf_op jit(solution)/shard_map/while/body/eval_jaxpr/ppermute | solution.py:19
  142.1 14.5 %collective-permute-start = (f32[2,64,128]{2,1,0:T(8,128)S(1)}, f32[2,64,128]{2,1,0:T(8,128)S(1)}, u32[]{:S(2)}, u32[]{:S(2)}) collective-permute-start(f32[2,64,128]{2,1,0:T(8,128)S(1)} %broadcast_select_fusion.2), channel_id=1, source_target_pairs={{0,4},{4,8},{8,12},{12,16},{16,20},{20,24},{24,28},{1,5},{5,9},{9,... | collective-permute-start | bytes 196616 | tf_op jit(solution)/shard_map/while/body/eval_jaxpr/ppermute | solution.py:27
  144.1 6.4 %collective-permute-start.3 = (f32[2,64,128]{2,1,0:T(8,128)S(1)}, f32[2,64,128]{2,1,0:T(8,128)S(1)}, u32[]{:S(2)}, u32[]{:S(2)}) collective-permute-start(f32[2,64,128]{2,1,0:T(8,128)S(1)} %get-tuple-element.476), channel_id=1, source_target_pairs={{4,0},{8,4},{12,8},{16,12},{20,16},{24,20},{28,24},{5,1},{9,5},{13... | collective-permute-start | bytes 196616 | tf_op jit(solution)/shard_map/while/body/eval_jaxpr/ppermute | solution.py:27
  150.8 12.1 %collective-permute-start.4 = (f32[1,64,128]{2,1,0:T(8,128)S(1)}, f32[1,64,128]{2,1,0:T(8,128)S(1)}, u32[]{:S(2)}, u32[]{:S(2)}) collective-permute-start(f32[1,64,128]{2,1,0:T(8,128)S(1)} %get-tuple-element.451), channel_id=1, source_target_pairs={{0,1},{1,2},{2,3},{4,5},{5,6},{6,7},{8,9},{9,10},{10,11},{12,13},{... | collective-permute-start | bytes 98312 | tf_op jit(solution)/shard_map/while/body/eval_jaxpr/ppermute | solution.py:16
  154.7 8.2 %collective-permute-start.5 = (f32[1,64,128]{2,1,0:T(8,128)S(1)}, f32[1,64,128]{2,1,0:T(8,128)S(1)}, u32[]{:S(2)}, u32[]{:S(2)}) collective-permute-start(f32[1,64,128]{2,1,0:T(8,128)S(1)} %get-tuple-element.452), channel_id=1, source_target_pairs={{1,0},{2,1},{3,2},{5,4},{6,5},{7,6},{9,8},{10,9},{11,10},{13,12},{... | collective-permute-start | bytes 98312 | tf_op jit(solution)/shard_map/while/body/eval_jaxpr/ppermute | solution.py:19
  157.0 6.5 %collective-permute-start.1 = (f32[1,2,64,128]{3,2,0,1:T(8,128)S(1)}, f32[1,2,64,128]{3,2,0,1:T(8,128)S(1)}, u32[]{:S(2)}, u32[]{:S(2)}) collective-permute-start(f32[1,2,64,128]{3,2,0,1:T(8,128)S(1)} %get-tuple-element.448), channel_id=1, source_target_pairs={{1,0},{2,1},{3,2},{5,4},{6,5},{7,6},{9,8},{10,9},{11,10},{13,12},{... | collective-permute-start | bytes 196616 | tf_op jit(solution)/shard_map/while/body/eval_jaxpr/ppermute | solution.py:19
  165.4 14.5 %collective-permute-start = (f32[2,64,128]{2,1,0:T(8,128)S(1)}, f32[2,64,128]{2,1,0:T(8,128)S(1)}, u32[]{:S(2)}, u32[]{:S(2)}) collective-permute-start(f32[2,64,128]{2,1,0:T(8,128)S(1)} %broadcast_select_fusion.2), channel_id=1, source_target_pairs={{0,4},{4,8},{8,12},{12,16},{16,20},{20,24},{24,28},{1,5},{5,9},{9,... | collective-permute-start | bytes 196616 | tf_op jit(solution)/shard_map/while/body/eval_jaxpr/ppermute | solution.py:27
  167.3 6.4 %collective-permute-start.3 = (f32[2,64,128]{2,1,0:T(8,128)S(1)}, f32[2,64,128]{2,1,0:T(8,128)S(1)}, u32[]{:S(2)}, u32[]{:S(2)}) collective-permute-start(f32[2,64,128]{2,1,0:T(8,128)S(1)} %get-tuple-element.476), channel_id=1, source_target_pairs={{4,0},{8,4},{12,8},{16,12},{20,16},{24,20},{28,24},{5,1},{9,5},{13... | collective-permute-start | bytes 196616 | tf_op jit(solution)/shard_map/while/body/eval_jaxpr/ppermute | solution.py:27
  174.0 12.1 %collective-permute-start.4 = (f32[1,64,128]{2,1,0:T(8,128)S(1)}, f32[1,64,128]{2,1,0:T(8,128)S(1)}, u32[]{:S(2)}, u32[]{:S(2)}) collective-permute-start(f32[1,64,128]{2,1,0:T(8,128)S(1)} %get-tuple-element.451), channel_id=1, source_target_pairs={{0,1},{1,2},{2,3},{4,5},{5,6},{6,7},{8,9},{9,10},{10,11},{12,13},{... | collective-permute-start | bytes 98312 | tf_op jit(solution)/shard_map/while/body/eval_jaxpr/ppermute | solution.py:16
  178.0 8.2 %collective-permute-start.5 = (f32[1,64,128]{2,1,0:T(8,128)S(1)}, f32[1,64,128]{2,1,0:T(8,128)S(1)}, u32[]{:S(2)}, u32[]{:S(2)}) collective-permute-start(f32[1,64,128]{2,1,0:T(8,128)S(1)} %get-tuple-element.452), channel_id=1, source_target_pairs={{1,0},{2,1},{3,2},{5,4},{6,5},{7,6},{9,8},{10,9},{11,10},{13,12},{... | collective-permute-start | bytes 98312 | tf_op jit(solution)/shard_map/while/body/eval_jaxpr/ppermute | solution.py:19
  180.3 6.5 %collective-permute-start.1 = (f32[1,2,64,128]{3,2,0,1:T(8,128)S(1)}, f32[1,2,64,128]{3,2,0,1:T(8,128)S(1)}, u32[]{:S(2)}, u32[]{:S(2)}) collective-permute-start(f32[1,2,64,128]{3,2,0,1:T(8,128)S(1)} %get-tuple-element.448), channel_id=1, source_target_pairs={{1,0},{2,1},{3,2},{5,4},{6,5},{7,6},{9,8},{10,9},{11,10},{13,12},{... | collective-permute-start | bytes 196616 | tf_op jit(solution)/shard_map/while/body/eval_jaxpr/ppermute | solution.py:19
  188.6 14.5 %collective-permute-start = (f32[2,64,128]{2,1,0:T(8,128)S(1)}, f32[2,64,128]{2,1,0:T(8,128)S(1)}, u32[]{:S(2)}, u32[]{:S(2)}) collective-permute-start(f32[2,64,128]{2,1,0:T(8,128)S(1)} %broadcast_select_fusion.2), channel_id=1, source_target_pairs={{0,4},{4,8},{8,12},{12,16},{16,20},{20,24},{24,28},{1,5},{5,9},{9,... | collective-permute-start | bytes 196616 | tf_op jit(solution)/shard_map/while/body/eval_jaxpr/ppermute | solution.py:27
  190.5 6.4 %collective-permute-start.3 = (f32[2,64,128]{2,1,0:T(8,128)S(1)}, f32[2,64,128]{2,1,0:T(8,128)S(1)}, u32[]{:S(2)}, u32[]{:S(2)}) collective-permute-start(f32[2,64,128]{2,1,0:T(8,128)S(1)} %get-tuple-element.476), channel_id=1, source_target_pairs={{4,0},{8,4},{12,8},{16,12},{20,16},{24,20},{28,24},{5,1},{9,5},{13... | collective-permute-start | bytes 196616 | tf_op jit(solution)/shard_map/while/body/eval_jaxpr/ppermute | solution.py:27
  197.3 12.1 %collective-permute-start.4 = (f32[1,64,128]{2,1,0:T(8,128)S(1)}, f32[1,64,128]{2,1,0:T(8,128)S(1)}, u32[]{:S(2)}, u32[]{:S(2)}) collective-permute-start(f32[1,64,128]{2,1,0:T(8,128)S(1)} %get-tuple-element.451), channel_id=1, source_target_pairs={{0,1},{1,2},{2,3},{4,5},{5,6},{6,7},{8,9},{9,10},{10,11},{12,13},{... | collective-permute-start | bytes 98312 | tf_op jit(solution)/shard_map/while/body/eval_jaxpr/ppermute | solution.py:16
  201.2 8.2 %collective-permute-start.5 = (f32[1,64,128]{2,1,0:T(8,128)S(1)}, f32[1,64,128]{2,1,0:T(8,128)S(1)}, u32[]{:S(2)}, u32[]{:S(2)}) collective-permute-start(f32[1,64,128]{2,1,0:T(8,128)S(1)} %get-tuple-element.452), channel_id=1, source_target_pairs={{1,0},{2,1},{3,2},{5,4},{6,5},{7,6},{9,8},{10,9},{11,10},{13,12},{... | collective-permute-start | bytes 98312 | tf_op jit(solution)/shard_map/while/body/eval_jaxpr/ppermute | solution.py:19
  203.5 6.5 %collective-permute-start.1 = (f32[1,2,64,128]{3,2,0,1:T(8,128)S(1)}, f32[1,2,64,128]{3,2,0,1:T(8,128)S(1)}, u32[]{:S(2)}, u32[]{:S(2)}) collective-permute-start(f32[1,2,64,128]{3,2,0,1:T(8,128)S(1)} %get-tuple-element.448), channel_id=1, source_target_pairs={{1,0},{2,1},{3,2},{5,4},{6,5},{7,6},{9,8},{10,9},{11,10},{13,12},{... | collective-permute-start | bytes 196616 | tf_op jit(solution)/shard_map/while/body/eval_jaxpr/ppermute | solution.py:19
  (12 other events, 53.0 us)
where the time goes:
time: 226 us; the launch traced here: 224 us
  starting transfers between devices  169 us (75%)
  waiting for transfers between devices  35.1 us (16%)
  matrix products  13.2 us (6%)
  local copies, waits for them, and re-layouts  3.74 us (2%)
    ppermute x19, starting transfers between devices, padded_2(): lax.ppermute(lax.slice_in_dim(block, block.shape[dim] - width, None, axis...  73.4 us
    ppermute x18, starting transfers between devices, from_behind(): return lax.ppermute(array, axis, pairs)  58.2 us
    ppermute x19, starting transfers between devices, padded_2(): lax.ppermute(lax.slice_in_dim(block, 0, width, axis=dim), axis, backward)  37.8 us
    ppermute x18, waiting for transfers between devices, from_behind(): return lax.ppermute(array, axis, pairs)  15.7 us
    ppermute x19, waiting for transfers between devices, padded_2(): lax.ppermute(lax.slice_in_dim(block, block.shape[dim] - width, None, axis...  15.3 us
    dot_general x9, matrix products, retreat(): return jnp.einsum('pikj,pkiw->kjw', blocks, shifted, precision=HIGHEST)  4.75 us
  transfers between devices with their start and end apart: 56, of which 20 were waited for; matrix products, arithmetic and copies ran while one was open for 5% of the time, Pallas kernels for 0%

commit v1 on v0

v1 whole, which is shorter than its diff:
```python
import functools
import math

import jax
import jax.numpy as jnp
from jax import lax
from jax.experimental import pallas as pl
from jax.experimental.pallas import tpu as pltpu
from jax.sharding import PartitionSpec as P

MESH = pl.DeviceIdType.MESH
F32 = jnp.float32
BF16 = jnp.bfloat16


def split(x):
    high = x.astype(BF16)
    low = (x - high.astype(F32)).astype(BF16)
    return high, low


def wide(x):
    return jnp.concatenate(split(x), axis=1)


def dot(a, b, contract):
    return lax.dot_general(a, b, (contract, ((), ())), preferred_element_type=F32)


def times(x_wide, y):
    pair = wide(y)
    both = dot(x_wide, jnp.concatenate([pair, pair], axis=0), ((1,), (0,)))
    n = y.shape[1]
    return both[:, :n] + both[:, n:]


def times_t(x_wide, y):
    high, low = split(y)
    rows = jnp.concatenate(
        [jnp.concatenate([high, high], axis=1), jnp.concatenate([low, low], axis=1)], axis=0
    )
    both = dot(x_wide, rows, ((1,), (1,)))
    n = y.shape[0]
    return both[:, :n] + both[:, n:]


def kernel(
    cols, secs, a_ref, b_ref, left_ref, right_ref, size_ref, out_ref,
    l_in, r_in, l_out, r_out, m_keep, x_keep, y_keep, a_wide, at_tall, weight, sizes, halo_sizes, prods, others,
    l_send, l_recv, r_send, r_recv, h_send, h_recv, k_send, k_recv,
):
    row_count = a_ref.shape[0]
    blk = a_ref.shape[3]
    width = b_ref.shape[3]
    rounds = cols.bit_length() - 1
    c = lax.axis_index("col")
    s = lax.axis_index("sec")
    below, above = s > 0, s < secs - 1
    before, after = c > 0, c < cols - 1
    low_rows, mid_rows, high_rows = pl.ds(0, blk), pl.ds(blk, 2 * blk), pl.ds(3 * blk, blk)

    def copy(src, dst, send, recv, dc, ds):
        return pltpu.make_async_remote_copy(
            src_ref=src, dst_ref=dst, send_sem=send, recv_sem=recv,
            device_id=(dc, ds), device_id_type=MESH,
        )

    barrier = pltpu.get_barrier_semaphore()
    count = jnp.int32(rounds)
    for k in range(rounds):
        partner = c + (1 << k) * (1 - 2 * ((c // (1 << k)) % 2))
        pl.semaphore_signal(barrier, inc=1, device_id=(partner, s), device_id_type=MESH)
    for dc, there in ((0, None), (-1, before), (1, after)):
        for ds, beside in ((0, None), (-1, below), (1, above)):
            if dc == 0 and ds == 0:
                continue
            if there is None:
                exists = beside
            elif beside is None:
                exists = there
            else:
                exists = there & beside
            count = count + exists.astype(jnp.int32)

            @pl.when(exists)
            def _(dc=dc, ds=ds):
                pl.semaphore_signal(barrier, inc=1, device_id=(c + dc, s + ds), device_id_type=MESH)

    sizes[0:8, :] = jnp.full((8, width), size_ref[0, 0].astype(F32), F32)
    sizes[8:16, :] = jnp.full((8, width), size_ref[0, 1].astype(F32), F32)
    norms = []
    for r in range(row_count):
        lower = b_ref[r, 0]
        norm = jnp.max(jnp.sum(jnp.abs(lower), axis=1, keepdims=True), axis=0, keepdims=True)
        norm = jnp.maximum(norm, 1e-30)
        norms.append(norm)
        prods[0, r] = lower / norm

    @pl.when(s == 0)
    def _():
        halo_sizes[0:8, :] = jnp.zeros((8, width), F32)
        r_in[:, low_rows, :] = jnp.zeros((row_count, blk, width), F32)
        l_in[:, low_rows, :] = jnp.zeros((row_count, blk, width), F32)

    @pl.when(s == secs - 1)
    def _():
        halo_sizes[8:16, :] = jnp.zeros((8, width), F32)
        r_in[:, high_rows, :] = jnp.zeros((row_count, blk, width), F32)
        l_in[:, high_rows, :] = jnp.zeros((row_count, blk, width), F32)

    pl.semaphore_wait(barrier, count)

    def size_up():
        return copy(sizes.at[8:16], halo_sizes.at[0:8], h_send.at[0], h_recv.at[0], c, s + 1)

    def size_down():
        return copy(sizes.at[0:8], halo_sizes.at[8:16], h_send.at[1], h_recv.at[1], c, s - 1)

    def right_copies(r, src, dc):
        return (
            copy(src.at[pl.ds(0, 2 * blk)], r_in.at[r, mid_rows], r_send.at[r, 0], r_recv.at[r, 0], dc, s),
            copy(src.at[pl.ds(0, blk)], r_in.at[r, high_rows], r_send.at[r, 1], r_recv.at[r, 1], dc, s - 1),
            copy(src.at[pl.ds(blk, blk)], r_in.at[r, low_rows], r_send.at[r, 2], r_recv.at[r, 2], dc, s + 1),
        )

    def left_copies(r):
        src = l_out.at[r]
        return (
            copy(src.at[mid_rows], l_in.at[r, mid_rows], l_send.at[r, 0], l_recv.at[r, 0], c + 1, s),
            copy(src.at[low_rows], l_in.at[r, high_rows], l_send.at[r, 1], l_recv.at[r, 1], c + 1, s - 1),
            copy(src.at[high_rows], l_in.at[r, low_rows], l_send.at[r, 2], l_recv.at[r, 2], c + 1, s + 1),
        )

    def product_copy(k, r):
        partner = c + (1 << k) * (1 - 2 * ((c // (1 << k)) % 2))
        return copy(prods.at[k, r], others.at[k, r], k_send.at[k, r], k_recv.at[k, r], partner, s)

    @pl.when(above)
    def _():
        size_up().start()

    @pl.when(below)
    def _():
        size_down().start()

    @pl.when(c == cols - 1)
    def _():
        for r in range(row_count):
            r_out[r] = right_ref[r].reshape(2 * blk, width)
            r_in[r, mid_rows, :] = right_ref[r].reshape(2 * blk, width)
            _, down, up = right_copies(r, r_out.at[r], c)

            @pl.when(below)
            def _():
                down.start()

            @pl.when(above)
            def _():
                up.start()

    @pl.when(c == 0)
    def _():
        for r in range(row_count):
            l_in[r, low_rows, :] = jnp.zeros((blk, width), F32)
            l_in[r, mid_rows, :] = left_ref[r].reshape(2 * blk, width)
            l_in[r, high_rows, :] = jnp.zeros((blk, width), F32)

    for r in range(row_count):
        product_copy(0, r).start()

    first = lax.broadcasted_iota(jnp.int32, (blk, 2 * blk), 1) < blk
    zero = jnp.zeros((blk, 2 * blk), F32)
    for r in range(row_count):
        parts = [a_ref[r, 0, p] for p in range(3)]
        matrix = jnp.concatenate(
            [
                jnp.where(first, parts[0], zero),
                jnp.where(first, parts[1], parts[0]),
                jnp.where(first, parts[2], parts[1]),
                jnp.where(first, zero, parts[2]),
            ],
            axis=0,
        )
        a_wide[r] = wide(matrix)
        at_tall[r] = jnp.concatenate(split(matrix.T), axis=0)

    @pl.when(below)
    def _():
        size_up().wait_recv()

    @pl.when(above)
    def _():
        size_down().wait_recv()

    place = lax.broadcasted_iota(jnp.int32, (blk, width), 0).astype(F32)
    for b, limit in enumerate((halo_sizes[0:1, :], sizes[0:1, :], sizes[8:9, :], halo_sizes[8:9, :])):
        live = (place < limit).astype(F32)
        for r in range(row_count):
            weight[r, b * blk : (b + 1) * blk, :] = live * norms[r]

    def left_step():
        for r in range(row_count):
            main, down, up = left_copies(r)

            @pl.when(before)
            def _():
                main.wait_recv()

            @pl.when(before & above)
            def _():
                down.wait_recv()

            @pl.when(before & below)
            def _():
                up.wait_recv()

            env = jnp.concatenate(
                [
                    l_in[r, blk : 2 * blk, :] + l_in[r, 0:blk, :],
                    l_in[r, 2 * blk : 3 * blk, :] + l_in[r, 3 * blk : 4 * blk, :],
                ],
                axis=0,
            )
            m_keep[r] = env

            @pl.when(after)
            def _():
                l_out[r] = times(a_wide[r], env) * weight[r]
                main.start()

                @pl.when(below)
                def _():
                    down.start()

                @pl.when(above)
                def _():
                    up.start()

    def right_step():
        for r in range(row_count):
            main, down, up = right_copies(r, r_out.at[r], c - 1)

            @pl.when(after)
            def _():
                main.wait_recv()

            @pl.when(above)
            def _():
                down.wait_recv()

            @pl.when(below)
            def _():
                up.wait_recv()

            env = r_in[r] * weight[r]
            x_keep[r] = env

            @pl.when(before)
            def _():
                @pl.when((c == cols - 1) & below)
                def _():
                    down.wait_send()

                @pl.when((c == cols - 1) & above)
                def _():
                    up.wait_send()

                both = dot(at_tall[r], wide(env), ((1,), (0,)))
                half = both[: 2 * blk] + both[2 * blk :]
                r_out[r] = half[:, :width] + half[:, width:]
                main.start()

                @pl.when(below)
                def _():
                    down.start()

                @pl.when(above)
                def _():
                    up.start()

    def product_round(k):
        upper = (c // (1 << k)) % 2 == 1
        for r in range(row_count):
            product_copy(k, r).wait_recv()
            mine, other = prods[k, r], others[k, r]
            x = jnp.where(upper, other, mine)
            y = jnp.where(upper, mine, other)
            prods[k + 1, r] = times(wide(x), y)
            if k + 1 < rounds:
                product_copy(k + 1, r).start()

    early = c < cols // 2

    def fold():
        @pl.when(early)
        def _():
            for r in range(row_count):
                y_keep[r] = times(wide(m_keep[r]), prods[rounds, r])

        @pl.when(jnp.logical_not(early))
        def _():
            for r in range(row_count):
                x_keep[r] = times_t(wide(x_keep[r]), prods[rounds, r])

    def slot(t, carry):
        @pl.when(c == t)
        def _():
            left_step()

        @pl.when(c == cols - 1 - t)
        def _():
            right_step()

        for k in range(rounds):

            @pl.when(t == k)
            def _():
                product_round(k)

        @pl.when(t == cols - 2)
        def _():
            fold()

        return carry

    lax.fori_loop(0, cols, slot, 0)

    scale = 1.0 / math.sqrt(width)
    for r in range(row_count):

        @pl.when(jnp.logical_not(early))
        def _():
            y_keep[r] = m_keep[r]

        full = times_t(wide(x_keep[r]), y_keep[r]) * scale
        for p in range(3):
            out_ref[r, 0, p] = jnp.where(
                first, full[p * blk : (p + 1) * blk], full[(p + 1) * blk : (p + 2) * blk]
            )

    @pl.when(above)
    def _():
        size_up().wait_send()

    @pl.when(below)
    def _():
        size_down().wait_send()

    for r in range(row_count):
        for k in range(rounds):
            product_copy(k, r).wait_send()
        for there, (main, down, up) in (
            (after, left_copies(r)),
            (before, right_copies(r, r_out.at[r], c - 1)),
        ):

            @pl.when(there)
            def _():
                main.wait_send()

            @pl.when(there & below)
            def _():
                down.wait_send()

            @pl.when(there & above)
            def _():
                up.wait_send()


def body(cols, secs, couplings, lower_sites, left_edge, right_edge, bond_sizes):
    row_count, _, _, blk, lanes = couplings.shape
    width = lower_sites.shape[3]
    rounds = cols.bit_length() - 1
    dma = pltpu.SemaphoreType.DMA
    vmem = pl.BlockSpec(memory_space=pltpu.VMEM)
    return pl.pallas_call(
        functools.partial(kernel, cols, secs),
        out_shape=jax.ShapeDtypeStruct(couplings.shape, F32),
        in_specs=[vmem] * 4 + [pl.BlockSpec(memory_space=pltpu.SMEM)],
        out_specs=vmem,
        scratch_shapes=[
            pltpu.VMEM((row_count, 4 * blk, width), F32),
            pltpu.VMEM((row_count, 4 * blk, width), F32),
            pltpu.VMEM((row_count, 4 * blk, width), F32),
            pltpu.VMEM((row_count, 2 * blk, width), F32),
            pltpu.VMEM((row_count, 2 * blk, width), F32),
            pltpu.VMEM((row_count, 4 * blk, width), F32),
            pltpu.VMEM((row_count, 2 * blk, width), F32),
            pltpu.VMEM((row_count, 4 * blk, 2 * lanes), BF16),
            pltpu.VMEM((row_count, 2 * lanes, 4 * blk), BF16),
            pltpu.VMEM((row_count, 4 * blk, width), F32),
            pltpu.VMEM((16, width), F32),
            pltpu.VMEM((16, width), F32),
            pltpu.VMEM((rounds + 1, row_count, width, width), F32),
            pltpu.VMEM((rounds, row_count, width, width), F32),
            dma((row_count, 3)),
            dma((row_count, 3)),
            dma((row_count, 3)),
            dma((row_count, 3)),
            dma((2,)),
            dma((2,)),
            dma((rounds, row_count)),
            dma((rounds, row_count)),
        ],
        compiler_params=pltpu.CompilerParams(
            collective_id=0, has_side_effects=True, vmem_limit_bytes=32 * 1024 * 1024
        ),
    )(couplings, lower_sites, left_edge, right_edge, bond_sizes)


def solution(mesh):
    in_specs = (
        P(None, "col", None, None, "sec"),
        P(None, "col", None, None),
        P(None, "sec", None, None),
        P(None, "sec", None, None),
        P("col", "sec"),
    )
    out_specs = P(None, "col", None, None, "sec")
    run = functools.partial(body, mesh.shape["col"], mesh.shape["sec"])
    return jax.shard_map(run, mesh=mesh, in_specs=in_specs, out_specs=out_specs, check_vma=False)
```

time: 226 us -> 39.3 us (0.17)
  the two profiles are of different devices: /device:TPU:20 before, /device:TPU:0 now
where the time goes in v1:
time: 39.3 us; the launch traced here: 39.1 us
  Pallas kernels  34.1 us (87%)
  local copies, waits for them, and re-layouts  4.97 us (13%)
    pallas_call x1, Pallas kernels, body(): pl.pallas_call(functools.partial(kernel, cols, secs), out_shape=jax.Shape...  34.1 us
    unnamed x11, local copies, waits for them, and re-layouts  4.97 us

profile of v1, /device:TPU:0, one launch (start us, length us, event | category | flops | bytes accessed | tf_op | source)
XLA Modules:
  0.0 39.1 jit_solution(3647067409044793762)
XLA Ops:
  0.0 0.0 copy-start
  0.0 0.9 %copy-done = f32[2,1,3,64,128]{4,3,2,1,0:T(8,128)S(1)} copy-done((f32[2,1,3,64,128]{4,3,2,1,0:T(8,128)S(1)}, f32[2,1,3,64,128]{4,3,2,1,0:T(8,128)}, u32[]{:S(2)}) %copy-start) | copy-done | bytes 196632
  0.9 0.0 copy-start.1
  0.9 0.9 %copy-done.1 = f32[2,1,128,128]{3,2,1,0:T(8,128)S(1)} copy-done((f32[2,1,128,128]{3,2,1,0:T(8,128)S(1)}, f32[2,1,128,128]{3,2,1,0:T(8,128)}, u32[]{:S(2)}) %copy-start.1) | copy-done | bytes 131096
  1.8 0.0 copy-start.2
  1.8 0.9 %copy-done.2 = f32[2,2,64,128]{3,2,1,0:T(8,128)S(1)} copy-done((f32[2,2,64,128]{3,2,1,0:T(8,128)S(1)}, f32[2,2,64,128]{3,2,1,0:T(8,128)}, u32[]{:S(2)}) %copy-start.2) | copy-done | bytes 131096
  2.7 0.0 copy-start.3
  2.7 0.9 %copy-done.3 = f32[2,2,64,128]{3,2,1,0:T(8,128)S(1)} copy-done((f32[2,2,64,128]{3,2,1,0:T(8,128)S(1)}, f32[2,2,64,128]{3,2,1,0:T(8,128)}, u32[]{:S(2)}) %copy-start.3) | copy-done | bytes 131096
  3.6 0.0 copy-start.4
  3.6 0.7 %copy-done.4 = s32[1,2]{1,0:T(1,128)S(1)} copy-done((s32[1,2]{1,0:T(1,128)S(1)}, s32[1,2]{1,0:T(1,128)}, u32[]{:S(2)}) %copy-start.4) | copy-done | bytes 32
  4.3 34.1 %shard_map.55 = f32[2,1,3,64,128]{4,3,2,1,0:T(8,128)S(1)} custom-call(f32[2,1,3,64,128]{4,3,2,1,0:T(8,128)S(1)} %copy-done, f32[2,1,128,128]{3,2,1,0:T(8,128)S(1)} %copy-done.1, f32[2,2,64,128]{3,2,1,0:T(8,128)S(1)} %copy-done.2, f32[2,2,64,128]{3,2,1,0:T(8,128)S(1)} %copy-done.3, s32[1,2]{1,0:T(1,128)S(1)} %copy-done.4), custom_call_target="tpu_custom_call" | custom-call | tf_op jit(solution)/shard_map/pallas_call | solution.py:376
  38.4 0.7 %copy.7 = f32[2,1,3,64,128]{4,3,2,1,0:T(8,128)} copy(f32[2,1,3,64,128]{4,3,2,1,0:T(8,128)S(1)} %shard_map.55) | data formatting | bytes 393216
Async XLA Ops:
  0.0 0.9 %copy-start = (f32[2,1,3,64,128]{4,3,2,1,0:T(8,128)S(1)}, f32[2,1,3,64,128]{4,3,2,1,0:T(8,128)}, u32[]{:S(2)}) copy-start(f32[2,1,3,64,128]{4,3,2,1,0:T(8,128)} %a_ref.1) | copy-start | bytes 589828
  0.9 0.9 %copy-start.1 = (f32[2,1,128,128]{3,2,1,0:T(8,128)S(1)}, f32[2,1,128,128]{3,2,1,0:T(8,128)}, u32[]{:S(2)}) copy-start(f32[2,1,128,128]{3,2,1,0:T(8,128)} %b_ref.1) | copy-start | bytes 393220
  1.8 0.9 %copy-start.2 = (f32[2,2,64,128]{3,2,1,0:T(8,128)S(1)}, f32[2,2,64,128]{3,2,1,0:T(8,128)}, u32[]{:S(2)}) copy-start(f32[2,2,64,128]{3,2,1,0:T(8,128)} %left_ref.1) | copy-start | bytes 393220
  2.7 0.9 %copy-start.3 = (f32[2,2,64,128]{3,2,1,0:T(8,128)S(1)}, f32[2,2,64,128]{3,2,1,0:T(8,128)}, u32[]{:S(2)}) copy-start(f32[2,2,64,128]{3,2,1,0:T(8,128)} %right_ref.1) | copy-start | bytes 393220
  3.6 0.7 %copy-start.4 = (s32[1,2]{1,0:T(1,128)S(1)}, s32[1,2]{1,0:T(1,128)}, u32[]{:S(2)}) copy-start(s32[1,2]{1,0:T(1,128)} %size_ref.1) | copy-start | bytes 28

commit v2 on v1

--- a/solution.py
+++ b/solution.py
@@ -45,9 +45,9 @@
 
 
 def kernel(
-    cols, secs, a_ref, b_ref, left_ref, right_ref, size_ref, out_ref,
+    cols, secs, a_hbm, b_hbm, left_hbm, right_hbm, size_hbm, out_ref, a_ref, b_ref, size_ref,
     l_in, r_in, l_out, r_out, m_keep, x_keep, y_keep, a_wide, at_tall, weight, sizes, halo_sizes, prods, others,
-    l_send, l_recv, r_send, r_recv, h_send, h_recv, k_send, k_recv,
+    l_send, l_recv, r_send, r_recv, h_send, h_recv, k_send, k_recv, local,
 ):
     row_count = a_ref.shape[0]
     blk = a_ref.shape[3]
@@ -64,6 +64,23 @@
             src_ref=src, dst_ref=dst, send_sem=send, recv_sem=recv,
             device_id=(dc, ds), device_id_type=MESH,
         )
+
+    load_a = pltpu.make_async_copy(a_hbm, a_ref, local.at[0])
+    load_b = pltpu.make_async_copy(b_hbm, b_ref, local.at[1])
+    load_size = pltpu.make_async_copy(size_hbm, size_ref, local.at[2])
+    load_left = pltpu.make_async_copy(left_hbm, l_in.at[:, mid_rows], local.at[3])
+    load_right = pltpu.make_async_copy(right_hbm, r_out, local.at[4])
+    load_size.start()
+    load_b.start()
+    load_a.start()
+
+    @pl.when(c == 0)
+    def _():
+        load_left.start()
+
+    @pl.when(c == cols - 1)
+    def _():
+        load_right.start()
 
     barrier = pltpu.get_barrier_semaphore()
     count = jnp.int32(rounds)
@@ -86,9 +103,11 @@
             def _(dc=dc, ds=ds):
                 pl.semaphore_signal(barrier, inc=1, device_id=(c + dc, s + ds), device_id_type=MESH)
 
+    load_size.wait()
     sizes[0:8, :] = jnp.full((8, width), size_ref[0, 0].astype(F32), F32)
     sizes[8:16, :] = jnp.full((8, width), size_ref[0, 1].astype(F32), F32)
     norms = []
+    load_b.wait()
     for r in range(row_count):
         lower = b_ref[r, 0]
         norm = jnp.max(jnp.sum(jnp.abs(lower), axis=1, keepdims=True), axis=0, keepdims=True)
@@ -145,9 +164,9 @@
 
     @pl.when(c == cols - 1)
     def _():
-        for r in range(row_count):
-            r_out[r] = right_ref[r].reshape(2 * blk, width)
-            r_in[r, mid_rows, :] = right_ref[r].reshape(2 * blk, width)
+        load_right.wait()
+        for r in range(row_count):
+            r_in[r, mid_rows, :] = r_out[r]
             _, down, up = right_copies(r, r_out.at[r], c)
 
             @pl.when(below)
@@ -162,14 +181,15 @@
     def _():
         for r in range(row_count):
             l_in[r, low_rows, :] = jnp.zeros((blk, width), F32)
-            l_in[r, mid_rows, :] = left_ref[r].reshape(2 * blk, width)
             l_in[r, high_rows, :] = jnp.zeros((blk, width), F32)
+        load_left.wait()
 
     for r in range(row_count):
         product_copy(0, r).start()
 
     first = lax.broadcasted_iota(jnp.int32, (blk, 2 * blk), 1) < blk
     zero = jnp.zeros((blk, 2 * blk), F32)
+    load_a.wait()
     for r in range(row_count):
         parts = [a_ref[r, 0, p] for p in range(3)]
         matrix = jnp.concatenate(
@@ -372,13 +392,18 @@
     width = lower_sites.shape[3]
     rounds = cols.bit_length() - 1
     dma = pltpu.SemaphoreType.DMA
+    left_edge = left_edge.reshape(row_count, lanes, width)
+    right_edge = right_edge.reshape(row_count, lanes, width)
     vmem = pl.BlockSpec(memory_space=pltpu.VMEM)
     return pl.pallas_call(
         functools.partial(kernel, cols, secs),
         out_shape=jax.ShapeDtypeStruct(couplings.shape, F32),
-        in_specs=[vmem] * 4 + [pl.BlockSpec(memory_space=pltpu.SMEM)],
+        in_specs=[pl.BlockSpec(memory_space=pltpu.HBM)] * 5,
         out_specs=vmem,
         scratch_shapes=[
+            pltpu.VMEM(couplings.shape, F32),
+            pltpu.VMEM(lower_sites.shape, F32),
+            pltpu.SMEM(bond_sizes.shape, jnp.int32),
             pltpu.VMEM((row_count, 4 * blk, width), F32),
             pltpu.VMEM((row_count, 4 * blk, width), F32),
             pltpu.VMEM((row_count, 4 * blk, width), F32),
@@ -401,9 +426,10 @@
             dma((2,)),
             dma((rounds, row_count)),
             dma((rounds, row_count)),
+            dma((5,)),
         ],
         compiler_params=pltpu.CompilerParams(
-            collective_id=0, has_side_effects=True, vmem_limit_bytes=32 * 1024 * 1024
+            collective_id=0, has_side_effects=True, vmem_limit_bytes=64 * 1024 * 1024 - 65536
         ),
     )(couplings, lower_sites, left_edge, right_edge, bond_sizes)
 

time: 39.3 us -> 36 us (0.916)
  local copies, waits for them, and re-layouts: 4.97 us -> 1.62 us
    unnamed x11 -> x1, local copies, waits for them, and re-layouts: 4.97 us -> 1.62 us
where the time goes in v2:
time: 36 us; the launch traced here: 35.8 us
  Pallas kernels  34.2 us (95%)
  local copies, waits for them, and re-layouts  1.62 us (4%)
    pallas_call x1, Pallas kernels, body(): pl.pallas_call(functools.partial(kernel, cols, secs), out_shape=jax.Shape...  34.2 us
    unnamed x1, local copies, waits for them, and re-layouts  1.62 us

profile of v2, /device:TPU:0, one launch (start us, length us, event | category | flops | bytes accessed | tf_op | source)
XLA Modules:
  0.0 35.8 jit_solution(7996814054156458132)
XLA Ops:
  0.0 34.2 %shard_map.55 = f32[2,1,3,64,128]{4,3,2,1,0:T(8,128)} custom-call(f32[2,1,3,64,128]{4,3,2,1,0:T(8,128)} %a_hbm.1, f32[2,1,128,128]{3,2,1,0:T(8,128)} %b_hbm.1, f32[2,128,128]{2,1,0:T(8,128)} %bitcast.2, f32[2,128,128]{2,1,0:T(8,128)} %bitcast.3, s32[1,2]{1,0:T(1,128)} %size_hbm.1), custom_call_target="tpu_custom_call" | custom-call | tf_op jit(solution)/shard_map/pallas_call | solution.py:398
  34.2 1.6 %copy.7 = f32[2,1,3,64,128]{4,3,2,1,0:T(8,128)} copy(f32[2,1,3,64,128]{4,3,2,1,0:T(8,128)} %shard_map.55) | data formatting | bytes 393216

commit v3 on v2

v3 whole, which is shorter than its diff:
```python
import functools
import math

import jax
import jax.numpy as jnp
from jax import lax
from jax.experimental import pallas as pl
from jax.experimental.pallas import tpu as pltpu
from jax.sharding import PartitionSpec as P

MESH = pl.DeviceIdType.MESH
F32 = jnp.float32
BF16 = jnp.bfloat16


def split(x):
    high = x.astype(BF16)
    low = (x - high.astype(F32)).astype(BF16)
    return high, low


def wide(x):
    return jnp.concatenate(split(x), axis=1)


def dot(a, b, contract):
    return lax.dot_general(a, b, (contract, ((), ())), preferred_element_type=F32)


def times(x_wide, y):
    pair = wide(y)
    both = dot(x_wide, jnp.concatenate([pair, pair], axis=0), ((1,), (0,)))
    n = y.shape[1]
    return both[:, :n] + both[:, n:]


def times_t(x_wide, y):
    high, low = split(y)
    rows = jnp.concatenate(
        [jnp.concatenate([high, high], axis=1), jnp.concatenate([low, low], axis=1)], axis=0
    )
    both = dot(x_wide, rows, ((1,), (1,)))
    n = y.shape[0]
    return both[:, :n] + both[:, n:]


def kernel(
    cols, secs, a_hbm, b_hbm, left_hbm, right_hbm, size_hbm, out_ref, a_ref, b_ref, size_ref,
    l_in, r_in, l_out, r_out, m_keep, x_keep, y_keep, a_wide, at_tall, weight, sizes, halo_sizes, halo_a, prods, others,
    l_send, l_recv, r_send, r_recv, h_send, h_recv, a_send, a_recv, k_send, k_recv, local,
):
    row_count = a_ref.shape[0]
    blk = a_ref.shape[3]
    width = b_ref.shape[3]
    rounds = cols.bit_length() - 1
    c = lax.axis_index("col")
    s = lax.axis_index("sec")
    below, above = s > 0, s < secs - 1
    before, after = c > 0, c < cols - 1
    odd = c % 2 == 1
    even = jnp.logical_not(odd)
    low_rows, mid_rows, high_rows = pl.ds(0, 2 * blk), pl.ds(2 * blk, 2 * blk), pl.ds(4 * blk, 2 * blk)
    near_rows = pl.ds(blk, 4 * blk)

    def copy(src, dst, send, recv, dc, ds):
        return pltpu.make_async_remote_copy(
            src_ref=src, dst_ref=dst, send_sem=send, recv_sem=recv,
            device_id=(dc, ds), device_id_type=MESH,
        )

    load_a = pltpu.make_async_copy(a_hbm, a_ref, local.at[0])
    load_b = pltpu.make_async_copy(b_hbm, b_ref, local.at[1])
    load_size = pltpu.make_async_copy(size_hbm, size_ref, local.at[2])
    load_left = pltpu.make_async_copy(left_hbm, l_in.at[:, mid_rows], local.at[3])
    load_right = pltpu.make_async_copy(right_hbm, r_in.at[:, mid_rows], local.at[4])
    load_size.start()
    load_b.start()
    load_a.start()

    @pl.when(c == 0)
    def _():
        load_left.start()

    @pl.when(c == cols - 1)
    def _():
        load_right.start()

    barrier = pltpu.get_barrier_semaphore()
    count = jnp.int32(rounds)
    for k in range(rounds):
        partner = c + (1 << k) * (1 - 2 * ((c // (1 << k)) % 2))
        pl.semaphore_signal(barrier, inc=1, device_id=(partner, s), device_id_type=MESH)
    for dc, there in ((0, None), (-1, before), (1, after)):
        for ds, beside in ((0, None), (-1, below), (1, above)):
            if dc == 0 and ds == 0:
                continue
            if there is None:
                exists = beside
            elif beside is None:
                exists = there
            else:
                exists = there & beside
            count = count + exists.astype(jnp.int32)

            @pl.when(exists)
            def _(dc=dc, ds=ds):
                pl.semaphore_signal(barrier, inc=1, device_id=(c + dc, s + ds), device_id_type=MESH)

    load_size.wait()
    sizes[0:8, :] = jnp.full((8, width), size_ref[0, 0].astype(F32), F32)
    sizes[8:16, :] = jnp.full((8, width), size_ref[0, 1].astype(F32), F32)
    norms = []
    load_b.wait()
    for r in range(row_count):
        lower = b_ref[r, 0]
        norm = jnp.max(jnp.sum(jnp.abs(lower), axis=1, keepdims=True), axis=0, keepdims=True)
        norm = jnp.maximum(norm, 1e-30)
        norms.append(norm)
        prods[0, r] = lower / norm

    def clear(ref, start, length):
        for r in range(row_count):
            ref[r, start : start + length, :] = jnp.zeros((length, width), F32)

    @pl.when(s == 0)
    def _():
        halo_sizes[0] = jnp.zeros((16, width), F32)
        halo_a[0] = jnp.zeros(halo_a.shape[1:], F32)

    @pl.when(s == secs - 1)
    def _():
        halo_sizes[1] = jnp.zeros((16, width), F32)
        halo_a[1] = jnp.zeros(halo_a.shape[1:], F32)

    for near, ref in ((odd, l_in), (even, r_in)):

        @pl.when(near)
        def _(ref=ref):
            clear(ref, 0, blk)
            clear(ref, 5 * blk, blk)

        @pl.when(jnp.logical_not(near) & (s == 0))
        def _(ref=ref):
            clear(ref, 0, 2 * blk)

        @pl.when(jnp.logical_not(near) & (s == secs - 1))
        def _(ref=ref):
            clear(ref, 4 * blk, 2 * blk)

    pl.semaphore_wait(barrier, count)

    def halo_copies(side, to):
        return [copy(sizes, halo_sizes.at[side], h_send.at[side], h_recv.at[side], c, to)] + [
            copy(a_ref.at[r], halo_a.at[side, r], a_send.at[side, r], a_recv.at[side, r], c, to)
            for r in range(row_count)
        ]

    def far_copies(src, dst, send, recv, to):
        return (
            copy(src, dst.at[mid_rows], send.at[0], recv.at[0], to, s),
            copy(src, dst.at[high_rows], send.at[1], recv.at[1], to, s - 1),
            copy(src, dst.at[low_rows], send.at[2], recv.at[2], to, s + 1),
        )

    def near_copy(src, dst, send, recv, to):
        return copy(src, dst.at[near_rows], send.at[0], recv.at[0], to, s)

    class Way:
        def __init__(self, src, dst, send, recv, to):
            self.args = (src, dst, send, recv)
            self.to = to

        def far(self, r, to=None, src=None):
            own, dst, send, recv = (ref.at[r] for ref in self.args)
            src = own.at[pl.ds(blk, 2 * blk)] if src is None else src
            return far_copies(src, dst, send, recv, self.to if to is None else to)

        def near(self, r):
            src, dst, send, recv = (ref.at[r] for ref in self.args)
            return near_copy(src, dst, send, recv, self.to)

    left = Way(l_out, l_in, l_send, l_recv, c + 1)
    right = Way(r_out, r_in, r_send, r_recv, c - 1)

    def edge_copies(way, r):
        return way.far(r, c, way.args[1].at[r, mid_rows])

    def sideways(copies, act, here=None):
        _, down, up = copies
        for exists, one in ((below, down), (above, up)):

            @pl.when(exists if here is None else exists & here)
            def _(one=one):
                act(one)

    def product_copy(k, r):
        partner = c + (1 << k) * (1 - 2 * ((c // (1 << k)) % 2))
        return copy(prods.at[k, r], others.at[k, r], k_send.at[k, r], k_recv.at[k, r], partner, s)

    load_a.wait()

    for exists, side, to in ((above, 0, s + 1), (below, 1, s - 1)):

        @pl.when(exists)
        def _(side=side, to=to):
            for one in halo_copies(side, to):
                one.start()

    for here, load, way in ((c == 0, load_left, left), (c == cols - 1, load_right, right)):

        @pl.when(here)
        def _(load=load, way=way):
            load.wait()
            for r in range(row_count):
                sideways(edge_copies(way, r), lambda one: one.start())

    for r in range(row_count):
        product_copy(0, r).start()

    first = lax.broadcasted_iota(jnp.int32, (blk, 2 * blk), 1) < blk
    zero = jnp.zeros((blk, 2 * blk), F32)

    def spread(of_first, of_second, height):
        return jnp.concatenate([jnp.where(first, of_first(n), of_second(n)) for n in range(height)], axis=0)

    for exists, side, to in ((below, 0, s - 1), (above, 1, s + 1)):

        @pl.when(exists)
        def _(side=side, to=to):
            for one in halo_copies(side, to):
                one.wait_recv()

    place = lax.broadcasted_iota(jnp.int32, (blk, width), 0).astype(F32)
    limits = [sizes[0:1, :], sizes[8:9, :]]
    limits = [halo_sizes[0, 0:1, :], halo_sizes[0, 8:9, :]] + limits
    limits = limits + [halo_sizes[1, 0:1, :], halo_sizes[1, 8:9, :]]
    for b, limit in enumerate(limits):
        live = (place < limit).astype(F32)
        for r in range(row_count):
            weight[r, b * blk : (b + 1) * blk, :] = live * norms[r]

    for r in range(row_count):

        def part(ref):
            return lambda p: ref[p] if 0 <= p <= 2 else zero

        low, own, high = part(halo_a.at[0, r, 0]), part(a_ref.at[r, 0]), part(halo_a.at[1, r, 0])
        groups = [
            spread(lambda n, g=g, one=one: one(n - 2 * g + 2), lambda n, g=g, one=one: one(n - 2 * g + 1), 4)
            for g, one in enumerate((low, own, high))
        ]
        a_wide[r] = wide(jnp.concatenate(groups, axis=1))
        inner = spread(lambda n: own(n - 1), lambda n: own(n - 2), 6)
        outer = spread(lambda n: high(n - 3), lambda n: low(n), 6)
        at_tall[r] = jnp.concatenate(split(jnp.concatenate([inner.T, outer.T], axis=0)), axis=0)

    def receive(way, r, near, start):
        @pl.when(near)
        def _():
            way.near(r).wait_recv()

        @pl.when(jnp.logical_not(near))
        def _():
            main, down, up = way.far(r)

            @pl.when(jnp.logical_not(start))
            def _():
                main.wait_recv()

            sideways((main, up, down), lambda one: one.wait_recv())

    def send(way, r, near):
        @pl.when(near)
        def _():
            way.near(r).start()

        @pl.when(jnp.logical_not(near))
        def _():
            copies = way.far(r)
            sideways(copies, lambda one: one.start())
            copies[0].start()

    def left_step():
        for r in range(row_count):
            receive(left, r, odd, c == 0)
            m_keep[r] = l_in[r, mid_rows, :]

            @pl.when(after)
            def _(r=r):
                l_out[r] = times(a_wide[r], l_in[r]) * weight[r, near_rows, :]
                send(left, r, even)

    def right_step():
        for r in range(row_count):
            receive(right, r, even, c == cols - 1)
            x_keep[r] = r_in[r, near_rows, :] * weight[r, near_rows, :]

            @pl.when(before)
            def _(r=r):
                both = dot(at_tall[r], wide(r_in[r] * weight[r]), ((1,), (0,)))
                half = both[: 4 * blk] + both[4 * blk :]
                half = half[:, :width] + half[:, width:]
                r_out[r, 0:blk, :] = half[3 * blk : 4 * blk]
                r_out[r, blk : 3 * blk, :] = half[0 : 2 * blk]
                r_out[r, 3 * blk : 4 * blk, :] = half[2 * blk : 3 * blk]
                send(right, r, odd)

    def product_round(k):
        upper = (c // (1 << k)) % 2 == 1
        for r in range(row_count):
            product_copy(k, r).wait_recv()
            mine, other = prods[k, r], others[k, r]
            x = jnp.where(upper, other, mine)
            y = jnp.where(upper, mine, other)
            prods[k + 1, r] = times(wide(x), y)
            if k + 1 < rounds:
                product_copy(k + 1, r).start()

    early = c < cols // 2

    def fold():
        @pl.when(early)
        def _():
            for r in range(row_count):
                y_keep[r] = times(wide(m_keep[r]), prods[rounds, r])

        @pl.when(jnp.logical_not(early))
        def _():
            for r in range(row_count):
                x_keep[r] = times_t(wide(x_keep[r]), prods[rounds, r])

    def slot(t, carry):
        @pl.when(c == t)
        def _():
            left_step()

        @pl.when(c == cols - 1 - t)
        def _():
            right_step()

        for k in range(rounds):

            @pl.when(t == 2 + 2 * k)
            def _():
                product_round(k)

        @pl.when(t == cols - 2)
        def _():
            fold()

        return carry

    lax.fori_loop(0, cols, slot, 0)

    scale = 1.0 / math.sqrt(width)
    for r in range(row_count):

        @pl.when(jnp.logical_not(early))
        def _():
            y_keep[r] = m_keep[r]

        full = times_t(wide(x_keep[r]), y_keep[r]) * scale
        for p in range(3):
            out_ref[r, 0, p] = jnp.where(
                first, full[p * blk : (p + 1) * blk], full[(p + 1) * blk : (p + 2) * blk]
            )

    for exists, side, to in ((above, 0, s + 1), (below, 1, s - 1)):

        @pl.when(exists)
        def _(side=side, to=to):
            for one in halo_copies(side, to):
                one.wait_send()

    for r in range(row_count):
        for k in range(rounds):
            product_copy(k, r).wait_send()
        for way, near, start, there in ((left, even, c == 0, after), (right, odd, c == cols - 1, before)):

            @pl.when(near & there)
            def _(way=way):
                way.near(r).wait_send()

            @pl.when(start)
            def _(way=way):
                sideways(edge_copies(way, r), lambda one: one.wait_send())

            @pl.when(jnp.logical_not(near) & there)
            def _(way=way):
                copies = way.far(r)
                copies[0].wait_send()
                sideways(copies, lambda one: one.wait_send())


def body(cols, secs, couplings, lower_sites, left_edge, right_edge, bond_sizes):
    row_count, _, _, blk, lanes = couplings.shape
    width = lower_sites.shape[3]
    rounds = cols.bit_length() - 1
    dma = pltpu.SemaphoreType.DMA
    left_edge = left_edge.reshape(row_count, lanes, width)
    right_edge = right_edge.reshape(row_count, lanes, width)
    vmem = pl.BlockSpec(memory_space=pltpu.VMEM)
    return pl.pallas_call(
        functools.partial(kernel, cols, secs),
        out_shape=jax.ShapeDtypeStruct(couplings.shape, F32),
        in_specs=[pl.BlockSpec(memory_space=pltpu.HBM)] * 5,
        out_specs=vmem,
        scratch_shapes=[
            pltpu.VMEM(couplings.shape, F32),
            pltpu.VMEM(lower_sites.shape, F32),
            pltpu.SMEM(bond_sizes.shape, jnp.int32),
            pltpu.VMEM((row_count, 6 * blk, width), F32),
            pltpu.VMEM((row_count, 6 * blk, width), F32),
            pltpu.VMEM((row_count, 4 * blk, width), F32),
            pltpu.VMEM((row_count, 4 * blk, width), F32),
            pltpu.VMEM((row_count, 2 * blk, width), F32),
            pltpu.VMEM((row_count, 4 * blk, width), F32),
            pltpu.VMEM((row_count, 2 * blk, width), F32),
            pltpu.VMEM((row_count, 4 * blk, 6 * lanes), BF16),
            pltpu.VMEM((row_count, 4 * lanes, 6 * blk), BF16),
            pltpu.VMEM((row_count, 6 * blk, width), F32),
            pltpu.VMEM((16, width), F32),
            pltpu.VMEM((2, 16, width), F32),
            pltpu.VMEM((2,) + couplings.shape, F32),
            pltpu.VMEM((rounds + 1, row_count, width, width), F32),
            pltpu.VMEM((rounds, row_count, width, width), F32),
            dma((row_count, 3)),
            dma((row_count, 3)),
            dma((row_count, 3)),
            dma((row_count, 3)),
            dma((2,)),
            dma((2,)),
            dma((2, row_count)),
            dma((2, row_count)),
            dma((rounds, row_count)),
            dma((rounds, row_count)),
            dma((5,)),
        ],
        compiler_params=pltpu.CompilerParams(
            collective_id=0, has_side_effects=True, vmem_limit_bytes=64 * 1024 * 1024 - 65536
        ),
    )(couplings, lower_sites, left_edge, right_edge, bond_sizes)


def solution(mesh):
    in_specs = (
        P(None, "col", None, None, "sec"),
        P(None, "col", None, None),
        P(None, "sec", None, None),
        P(None, "sec", None, None),
        P("col", "sec"),
    )
    out_specs = P(None, "col", None, None, "sec")
    run = functools.partial(body, mesh.shape["col"], mesh.shape["sec"])
    return jax.shard_map(run, mesh=mesh, in_specs=in_specs, out_specs=out_specs, check_vma=False)
```

time: 36 us -> 38 us (1.056)
  Pallas kernels: 34.2 us -> 36.3 us
    pallas_call x1, Pallas kernels: 34.2 us -> 36.3 us  [body(): pl.pallas_call(functools.partial(kernel, cols, secs), out_shape=jax.Shape...]
where the time goes in v3:
time: 38 us; the launch traced here: 37.9 us
  Pallas kernels  36.3 us (96%)
  local copies, waits for them, and re-layouts  1.62 us (4%)
    pallas_call x1, Pallas kernels, body(): pl.pallas_call(functools.partial(kernel, cols, secs), out_shape=jax.Shape...  36.3 us
    unnamed x1, local copies, waits for them, and re-layouts  1.62 us

profile of v3, /device:TPU:0, one launch (start us, length us, event | category | flops | bytes accessed | tf_op | source)
XLA Modules:
  0.0 37.9 jit_solution(11725709110711078893)
XLA Ops:
  0.0 36.3 %shard_map.55 = f32[2,1,3,64,128]{4,3,2,1,0:T(8,128)} custom-call(f32[2,1,3,64,128]{4,3,2,1,0:T(8,128)} %a_hbm.1, f32[2,1,128,128]{3,2,1,0:T(8,128)} %b_hbm.1, f32[2,128,128]{2,1,0:T(8,128)} %bitcast.2, f32[2,128,128]{2,1,0:T(8,128)} %bitcast.3, s32[1,2]{1,0:T(1,128)} %size_hbm.1), custom_call_target="tpu_custom_call" | custom-call | tf_op jit(solution)/shard_map/pallas_call | solution.py:403
  36.3 1.6 %copy.7 = f32[2,1,3,64,128]{4,3,2,1,0:T(8,128)} copy(f32[2,1,3,64,128]{4,3,2,1,0:T(8,128)} %shard_map.55) | data formatting | bytes 393216

commit v4 on v2

--- a/solution.py
+++ b/solution.py
@@ -246,15 +246,15 @@
             @pl.when(after)
             def _():
                 l_out[r] = times(a_wide[r], env) * weight[r]
+                @pl.when(below)
+                def _():
+                    down.start()
+
+                @pl.when(above)
+                def _():
+                    up.start()
+
                 main.start()
-
-                @pl.when(below)
-                def _():
-                    down.start()
-
-                @pl.when(above)
-                def _():
-                    up.start()
 
     def right_step():
         for r in range(row_count):
@@ -288,15 +288,15 @@
                 both = dot(at_tall[r], wide(env), ((1,), (0,)))
                 half = both[: 2 * blk] + both[2 * blk :]
                 r_out[r] = half[:, :width] + half[:, width:]
+                @pl.when(below)
+                def _():
+                    down.start()
+
+                @pl.when(above)
+                def _():
+                    up.start()
+
                 main.start()
-
-                @pl.when(below)
-                def _():
-                    down.start()
-
-                @pl.when(above)
-                def _():
-                    up.start()
 
     def product_round(k):
         upper = (c // (1 << k)) % 2 == 1
@@ -333,7 +333,7 @@
 
         for k in range(rounds):
 
-            @pl.when(t == k)
+            @pl.when(t == 2 + 2 * k)
             def _():
                 product_round(k)
 

time: 36 us -> 35.7 us (level)
  no operation moved by 1% of the time
where the time goes in v4:
time: 35.7 us; the launch traced here: 35.6 us
  Pallas kernels  33.9 us (95%)
  local copies, waits for them, and re-layouts  1.62 us (5%)
    pallas_call x1, Pallas kernels, body(): pl.pallas_call(functools.partial(kernel, cols, secs), out_shape=jax.Shape...  33.9 us
    unnamed x1, local copies, waits for them, and re-layouts  1.62 us

profile of v4, /device:TPU:0, one launch (start us, length us, event | category | flops | bytes accessed | tf_op | source)
XLA Modules:
  0.0 35.6 jit_solution(7308770144857750229)
XLA Ops:
  0.0 33.9 %shard_map.55 = f32[2,1,3,64,128]{4,3,2,1,0:T(8,128)} custom-call(f32[2,1,3,64,128]{4,3,2,1,0:T(8,128)} %a_hbm.1, f32[2,1,128,128]{3,2,1,0:T(8,128)} %b_hbm.1, f32[2,128,128]{2,1,0:T(8,128)} %bitcast.2, f32[2,128,128]{2,1,0:T(8,128)} %bitcast.3, s32[1,2]{1,0:T(1,128)} %size_hbm.1), custom_call_target="tpu_custom_call" | custom-call | tf_op jit(solution)/shard_map/pallas_call | solution.py:398
  33.9 1.6 %copy.7 = f32[2,1,3,64,128]{4,3,2,1,0:T(8,128)} copy(f32[2,1,3,64,128]{4,3,2,1,0:T(8,128)} %shard_map.55) | data formatting | bytes 393216

commit v5 on v3

--- a/solution.py
+++ b/solution.py
@@ -199,20 +199,21 @@
 
     load_a.wait()
 
-    for exists, side, to in ((above, 0, s + 1), (below, 1, s - 1)):
-
-        @pl.when(exists)
-        def _(side=side, to=to):
-            for one in halo_copies(side, to):
-                one.start()
-
-    for here, load, way in ((c == 0, load_left, left), (c == cols - 1, load_right, right)):
-
-        @pl.when(here)
-        def _(load=load, way=way):
-            load.wait()
-            for r in range(row_count):
-                sideways(edge_copies(way, r), lambda one: one.start())
+    for k in range(1 + row_count):
+        for exists, side, to in ((above, 0, s + 1), (below, 1, s - 1)):
+
+            @pl.when(exists)
+            def _(side=side, to=to):
+                halo_copies(side, to)[k].start()
+
+        if k > 0:
+            for here, load, way in ((c == 0, load_left, left), (c == cols - 1, load_right, right)):
+
+                @pl.when(here)
+                def _(load=load, way=way):
+                    if k == 1:
+                        load.wait()
+                    sideways(edge_copies(way, k - 1), lambda one: one.start())
 
     for r in range(row_count):
         product_copy(0, r).start()
@@ -223,12 +224,14 @@
     def spread(of_first, of_second, height):
         return jnp.concatenate([jnp.where(first, of_first(n), of_second(n)) for n in range(height)], axis=0)
 
-    for exists, side, to in ((below, 0, s - 1), (above, 1, s + 1)):
-
-        @pl.when(exists)
-        def _(side=side, to=to):
-            for one in halo_copies(side, to):
-                one.wait_recv()
+    def arrive(k):
+        for exists, side, to in ((below, 0, s - 1), (above, 1, s + 1)):
+
+            @pl.when(exists)
+            def _(side=side, to=to):
+                halo_copies(side, to)[k].wait_recv()
+
+    arrive(0)
 
     place = lax.broadcasted_iota(jnp.int32, (blk, width), 0).astype(F32)
     limits = [sizes[0:1, :], sizes[8:9, :]]
@@ -239,7 +242,8 @@
         for r in range(row_count):
             weight[r, b * blk : (b + 1) * blk, :] = live * norms[r]
 
-    for r in range(row_count):
+    def prepare(r):
+        arrive(1 + r)
 
         def part(ref):
             return lambda p: ref[p] if 0 <= p <= 2 else zero
@@ -280,8 +284,8 @@
             sideways(copies, lambda one: one.start())
             copies[0].start()
 
-    def left_step():
-        for r in range(row_count):
+    def left_step(rows=range(row_count)):
+        for r in rows:
             receive(left, r, odd, c == 0)
             m_keep[r] = l_in[r, mid_rows, :]
 
@@ -290,8 +294,8 @@
                 l_out[r] = times(a_wide[r], l_in[r]) * weight[r, near_rows, :]
                 send(left, r, even)
 
-    def right_step():
-        for r in range(row_count):
+    def right_step(rows=range(row_count)):
+        for r in rows:
             receive(right, r, even, c == cols - 1)
             x_keep[r] = r_in[r, near_rows, :] * weight[r, near_rows, :]
 
@@ -350,7 +354,18 @@
 
         return carry
 
-    lax.fori_loop(0, cols, slot, 0)
+    for r in range(row_count):
+        prepare(r)
+
+        @pl.when(c == 0)
+        def _(r=r):
+            left_step([r])
+
+        @pl.when(c == cols - 1)
+        def _(r=r):
+            right_step([r])
+
+    lax.fori_loop(1, cols, slot, 0)
 
     scale = 1.0 / math.sqrt(width)
     for r in range(row_count):

time: 38 us -> 38.4 us (1.011)
    pallas_call x1, Pallas kernels: 36.3 us -> 36.6 us  [body(): pl.pallas_call(functools.partial(kernel, cols, secs), out_shape=jax.Shape...]
where the time goes in v5:
time: 38.4 us; the launch traced here: 38.3 us
  Pallas kernels  36.6 us (95%)
  local copies, waits for them, and re-layouts  1.62 us (4%)
    pallas_call x1, Pallas kernels, body(): pl.pallas_call(functools.partial(kernel, cols, secs), out_shape=jax.Shape...  36.6 us
    unnamed x1, local copies, waits for them, and re-layouts  1.62 us

profile of v5, /device:TPU:0, one launch (start us, length us, event | category | flops | bytes accessed | tf_op | source)
XLA Modules:
  0.0 38.3 jit_solution(191357556710884083)
XLA Ops:
  0.0 36.6 %shard_map.55 = f32[2,1,3,64,128]{4,3,2,1,0:T(8,128)} custom-call(f32[2,1,3,64,128]{4,3,2,1,0:T(8,128)} %a_hbm.1, f32[2,1,128,128]{3,2,1,0:T(8,128)} %b_hbm.1, f32[2,128,128]{2,1,0:T(8,128)} %bitcast.2, f32[2,128,128]{2,1,0:T(8,128)} %bitcast.3, s32[1,2]{1,0:T(1,128)} %size_hbm.1), custom_call_target="tpu_custom_call" | custom-call | tf_op jit(solution)/shard_map/pallas_call | solution.py:418
  36.6 1.6 %copy.7 = f32[2,1,3,64,128]{4,3,2,1,0:T(8,128)} copy(f32[2,1,3,64,128]{4,3,2,1,0:T(8,128)} %shard_map.55) | data formatting | bytes 393216

commit v6 on v4

--- a/solution.py
+++ b/solution.py
@@ -345,14 +345,13 @@
 
     lax.fori_loop(0, cols, slot, 0)
 
-    scale = 1.0 / math.sqrt(width)
     for r in range(row_count):
 
         @pl.when(jnp.logical_not(early))
         def _():
             y_keep[r] = m_keep[r]
 
-        full = times_t(wide(x_keep[r]), y_keep[r]) * scale
+        full = times_t(wide(x_keep[r]), y_keep[r])
         for p in range(3):
             out_ref[r, 0, p] = jnp.where(
                 first, full[p * blk : (p + 1) * blk], full[(p + 1) * blk : (p + 2) * blk]
@@ -395,7 +394,7 @@
     left_edge = left_edge.reshape(row_count, lanes, width)
     right_edge = right_edge.reshape(row_count, lanes, width)
     vmem = pl.BlockSpec(memory_space=pltpu.VMEM)
-    return pl.pallas_call(
+    gradient = pl.pallas_call(
         functools.partial(kernel, cols, secs),
         out_shape=jax.ShapeDtypeStruct(couplings.shape, F32),
         in_specs=[pl.BlockSpec(memory_space=pltpu.HBM)] * 5,
@@ -432,6 +431,7 @@
             collective_id=0, has_side_effects=True, vmem_limit_bytes=64 * 1024 * 1024 - 65536
         ),
     )(couplings, lower_sites, left_edge, right_edge, bond_sizes)
+    return gradient * (1.0 / math.sqrt(width))
 
 
 def solution(mesh):

time: 35.7 us -> 35.7 us (level)
  other arithmetic: 0 us -> 1.62 us
  local copies, waits for them, and re-layouts: 1.62 us -> 0 us
    mul x0 -> x1, other arithmetic: none -> 1.62 us  [body(): return gradient * (1.0 / math.sqrt(width))]
    unnamed x1 -> x0, local copies, waits for them, and re-layouts: 1.62 us -> none
where the time goes in v6:
time: 35.7 us; the launch traced here: 35.6 us
  Pallas kernels  33.9 us (95%)
  other arithmetic  1.62 us (5%)
    pallas_call x1, Pallas kernels, body(): pl.pallas_call(functools.partial(kernel, cols, secs), out_shape=jax.Shape...  33.9 us
    mul x1, other arithmetic, body(): return gradient * (1.0 / math.sqrt(width))  1.62 us

profile of v6, /device:TPU:0, one launch (start us, length us, event | category | flops | bytes accessed | tf_op | source)
XLA Modules:
  0.0 35.6 jit_solution(9598783829364179832)
XLA Ops:
  0.0 33.9 %shard_map.55 = f32[2,1,3,64,128]{4,3,2,1,0:T(8,128)} custom-call(f32[2,1,3,64,128]{4,3,2,1,0:T(8,128)} %a_hbm.1, f32[2,1,128,128]{3,2,1,0:T(8,128)} %b_hbm.1, f32[2,128,128]{2,1,0:T(8,128)} %bitcast.2, f32[2,128,128]{2,1,0:T(8,128)} %bitcast.3, s32[1,2]{1,0:T(1,128)} %size_hbm.1), custom_call_target="tpu_custom_call" | custom-call | tf_op jit(solution)/shard_map/pallas_call | solution.py:397
  33.9 1.6 %broadcast_multiply_fusion = f32[2,1,3,64,128]{4,3,2,1,0:T(8,128)} fusion(f32[2,1,3,64,128]{4,3,2,1,0:T(8,128)} %shard_map.55), kind=kLoop, calls=%fused_computation | loop fusion | flops 49152 | bytes 393216 | tf_op jit(solution)/shard_map/mul | solution.py:434
